TPU v7x, 256 devices: a whole 4x4x8 slice. The times are simulated.
256 devices in a mesh: seq: 128 (over y, z, x_hi, core), head: 2 (over x_lo).
Axes of the slice: x: 4 (x_hi: 2, x_lo: 2; x = x_hi * 2 + x_lo), y: 4, z: 8, core: 2. Of those that a mesh axis runs over, the one named last changes fastest.
Arguments:
- queries: bfloat16 [131072, 1024], P('seq', 'head'), may hold values from -6 to 6
- key_rows: bfloat16 [131072, 1024], P('seq', 'head'), may hold values from -6 to 6
- value_rows: bfloat16 [131072, 1024], P('seq', 'head'), may hold values from -24 to 24
- out_proj: bfloat16 [1024, 1024], P('head'), may hold values from -0.1875 to 0.1875
- grad_out: bfloat16 [131072, 1024], P('seq', 'head'), may hold values from -24 to 24
- band_blocks: int32 [2048], P('seq'), may hold values from 1 to 9, as said below
- column_reach: int32 [2048], P('seq'), may hold values from 2 to 256, as said below
Outputs:
- output: bfloat16 [131072, 1024], P('seq', 'head')
- query_grad: bfloat16 [131072, 1024], P('seq', 'head')
- key_grad: bfloat16 [131072, 1024], P('seq', 'head')
- value_grad: bfloat16 [131072, 1024], P('seq', 'head')
- proj_grad: float32 [1024, 1024], P('head', 'seq')
Inputs may be any that keep to these rules, and one draw needn't show every extreme that they name: `band_blocks`: the value 9 occurs in every draw. `column_reach`: the value 256 occurs in every draw.
All inputs are finite; a program needn't handle non-finite values.
Results may differ from a plain program's by a relative error of at most 0.015.
Values may be sent and summed in bfloat16 or wider, within the bound.
A program may use at most 128 MiB of HBM per device.

v0:
```python
import math

import jax
import jax.numpy as jnp
from jax import lax
from jax.sharding import PartitionSpec as P

HEAD_DIM = 64
STRIDE = 512
BLOCK = 64


MASKED = -1e30


def passed_along(block, axis, distance):
    devices = range(lax.axis_size(axis))
    route = [(i - distance, i) for i in devices if i - distance in devices]
    return lax.ppermute(block, axis, route)


def masked_scores(query_part, key_part, allowed):
    raw_scores = jnp.einsum(
        "nbhd,mbhd->bhnm", query_part, key_part, preferred_element_type=jnp.float32
    )
    raw_scores = raw_scores * query_part.shape[-1] ** (-0.5)
    return jnp.where(allowed[:, None], raw_scores, MASKED)


def attend(query_part, key_part, value_part, allowed):
    scores = masked_scores(query_part, key_part, allowed)
    highest = jnp.max(scores, axis=-1, keepdims=True)
    totals = jnp.sum(jnp.exp(scores - highest), axis=-1, keepdims=True)
    log_total = highest + jnp.log(totals)
    weights = jnp.exp(scores - log_total).astype(jnp.bfloat16)
    result = jnp.einsum("bhnm,mbhd->nbhd", weights, value_part, preferred_element_type=jnp.float32)
    return (result.astype(jnp.bfloat16), log_total[..., 0])


def attend_back(query_part, key_part, value_part, allowed, log_total, d_result, result):
    factor = query_part.shape[-1] ** (-0.5)
    scores = masked_scores(query_part, key_part, allowed)
    weights_full = jnp.exp(scores - log_total[..., None])
    row_inner = jnp.einsum("nbhd,nbhd->bhn", d_result, result, preferred_element_type=jnp.float32)
    d_weights = jnp.einsum(
        "nbhd,mbhd->bhnm", d_result, value_part, preferred_element_type=jnp.float32
    )
    d_scores = (weights_full * (d_weights - row_inner[..., None])).astype(jnp.bfloat16)
    d_query = (
        jnp.einsum("bhnm,mbhd->nbhd", d_scores, key_part, preferred_element_type=jnp.float32)
        * factor
    )
    d_key = (
        jnp.einsum("bhnm,nbhd->mbhd", d_scores, query_part, preferred_element_type=jnp.float32)
        * factor
    )
    d_value = jnp.einsum(
        "bhnm,nbhd->mbhd",
        weights_full.astype(jnp.bfloat16),
        d_result,
        preferred_element_type=jnp.float32,
    )
    return (d_query, d_key, d_value)


def local(queries, key_rows, value_rows, out_proj, grad_out, band_blocks, column_reach):
    tokens_dev, local_width = queries.shape
    half_width = local_width // 2
    head_dim = HEAD_DIM
    heads_half = half_width // head_dim
    stride = STRIDE
    block_len = BLOCK
    rows_dev = tokens_dev // stride
    seq_devices = lax.axis_size("seq")
    seq_index = lax.axis_index("seq")
    offset = seq_index * tokens_dev
    all_rows = rows_dev * seq_devices
    cols_dev = stride // seq_devices
    window_shape = (stride, 1, heads_half, head_dim)
    band_query = queries[:, :half_width]
    band_key = key_rows[:, :half_width]
    band_value = value_rows[:, :half_width]
    rim_pair = passed_along(
        jnp.stack([band_key[tokens_dev - stride :], band_value[tokens_dev - stride :]]), "seq", 1
    )
    key_ext = jnp.concatenate([rim_pair[0], band_key], axis=0).reshape(
        stride + tokens_dev, 1, heads_half, head_dim
    )
    value_ext = jnp.concatenate([rim_pair[1], band_value], axis=0).reshape(
        stride + tokens_dev, 1, heads_half, head_dim
    )
    band_reach = jnp.broadcast_to(band_blocks[:, None], (band_blocks.shape[0], block_len)).reshape(
        tokens_dev
    )

    def band_mask(window):
        begin_at = window * stride
        pos_query = offset + begin_at + jnp.arange(stride, dtype=jnp.int32)
        pos_key = offset + begin_at - stride + jnp.arange(2 * stride, dtype=jnp.int32)
        blocks_apart = pos_query[:, None] // block_len - pos_key[None, :] // block_len
        allowed = (
            (pos_key[None, :] <= pos_query[:, None])
            & (pos_key[None, :] >= 0)
            & (blocks_apart < band_reach[begin_at : begin_at + stride, None])
        )
        return allowed[None]

    band_results = []
    band_totals = []
    for window in range(rows_dev):
        begin_at = window * stride
        query_part = band_query[begin_at : begin_at + stride].reshape(window_shape)
        result, log_total = attend(
            query_part,
            key_ext[begin_at : begin_at + 2 * stride],
            value_ext[begin_at : begin_at + 2 * stride],
            band_mask(window),
        )
        band_results.append(result)
        band_totals.append(log_total)

    def column_layout(matrix):
        return matrix[:, half_width:].reshape(rows_dev, stride, half_width)

    column_shape = (all_rows, cols_dev, heads_half, head_dim)
    col_query, col_key, col_value = (
        lax.all_to_all(column_layout(queries), "seq", split_axis=1, concat_axis=0, tiled=True),
        lax.all_to_all(column_layout(key_rows), "seq", split_axis=1, concat_axis=0, tiled=True),
        lax.all_to_all(column_layout(value_rows), "seq", split_axis=1, concat_axis=0, tiled=True),
    )
    col_query = col_query.reshape(column_shape)
    col_key = col_key.reshape(column_shape)
    col_value = col_value.reshape(column_shape)
    reach_all = lax.all_gather(column_reach, "seq", axis=0, tiled=True).reshape(
        all_rows, stride // block_len
    )
    col_ids = seq_index * cols_dev + jnp.arange(cols_dev, dtype=jnp.int32)
    pick_table = (
        jnp.arange(stride // block_len, dtype=jnp.int32)[:, None] == (col_ids // block_len)[None, :]
    ).astype(jnp.int32)
    reach_cols = jnp.sum(reach_all[:, :, None] * pick_table[None], axis=1)
    row_ids = jnp.arange(all_rows, dtype=jnp.int32)
    rows_apart = row_ids[:, None] - row_ids[None, :]
    col_mask = (rows_apart[None] >= 0) & (rows_apart[None] < jnp.transpose(reach_cols)[:, :, None])
    col_result, col_total = attend(col_query, col_key, col_value, col_mask)
    row_result = lax.all_to_all(
        col_result.reshape(all_rows, cols_dev, half_width),
        "seq",
        split_axis=0,
        concat_axis=1,
        tiled=True,
    )
    attended = jnp.concatenate(
        [
            jnp.concatenate(band_results, axis=0).reshape(tokens_dev, half_width),
            row_result.reshape(tokens_dev, half_width),
        ],
        axis=1,
    )
    partial_out = jnp.dot(attended, out_proj, preferred_element_type=jnp.float32)
    output = lax.psum_scatter(partial_out, "head", scatter_dimension=1, tiled=True).astype(
        jnp.bfloat16
    )
    grad_all = lax.all_gather(grad_out, "head", axis=1, tiled=True)
    d_attended = jnp.einsum(
        "tc,fc->tf", grad_all, out_proj, preferred_element_type=jnp.float32
    ).astype(jnp.bfloat16)
    proj_term = jnp.einsum("tf,tc->fc", attended, grad_all, preferred_element_type=jnp.float32)
    proj_grad = lax.psum_scatter(proj_term, "seq", scatter_dimension=1, tiled=True) * (
        1.0 / math.sqrt(tokens_dev * seq_devices)
    )
    d_band = d_attended[:, :half_width]
    key_grad_ext = jnp.zeros((stride + tokens_dev, 1, heads_half, head_dim), jnp.float32)
    value_grad_ext = jnp.zeros((stride + tokens_dev, 1, heads_half, head_dim), jnp.float32)
    query_band_grads = []
    for window in range(rows_dev):
        begin_at = window * stride
        query_part = band_query[begin_at : begin_at + stride].reshape(window_shape)
        d_part = d_band[begin_at : begin_at + stride].reshape(window_shape)
        d_query, d_key, d_value = attend_back(
            query_part,
            key_ext[begin_at : begin_at + 2 * stride],
            value_ext[begin_at : begin_at + 2 * stride],
            band_mask(window),
            band_totals[window],
            d_part,
            band_results[window],
        )
        query_band_grads.append(d_query.astype(jnp.bfloat16))
        key_grad_ext = key_grad_ext.at[begin_at : begin_at + 2 * stride].add(d_key)
        value_grad_ext = value_grad_ext.at[begin_at : begin_at + 2 * stride].add(d_value)
    rim_back = passed_along(
        jnp.stack(
            [
                key_grad_ext[:stride].reshape(stride, half_width),
                value_grad_ext[:stride].reshape(stride, half_width),
            ]
        ).astype(jnp.bfloat16),
        "seq",
        -1,
    ).astype(jnp.float32)
    key_band_grad = (
        key_grad_ext[stride:]
        .reshape(tokens_dev, half_width)
        .at[tokens_dev - stride :]
        .add(rim_back[0])
    )
    value_band_grad = (
        value_grad_ext[stride:]
        .reshape(tokens_dev, half_width)
        .at[tokens_dev - stride :]
        .add(rim_back[1])
    )
    d_column = lax.all_to_all(
        d_attended[:, half_width:].reshape(rows_dev, stride, half_width),
        "seq",
        split_axis=1,
        concat_axis=0,
        tiled=True,
    ).reshape(column_shape)
    col_dq, col_dk, col_dv = attend_back(
        col_query, col_key, col_value, col_mask, col_total, d_column, col_result
    )
    flat_shape = (all_rows, cols_dev, half_width)
    row_grads = (
        lax.all_to_all(
            col_dq.astype(jnp.bfloat16).reshape(flat_shape),
            "seq",
            split_axis=0,
            concat_axis=1,
            tiled=True,
        ),
        lax.all_to_all(
            col_dk.astype(jnp.bfloat16).reshape(flat_shape),
            "seq",
            split_axis=0,
            concat_axis=1,
            tiled=True,
        ),
        lax.all_to_all(
            col_dv.astype(jnp.bfloat16).reshape(flat_shape),
            "seq",
            split_axis=0,
            concat_axis=1,
            tiled=True,
        ),
    )

    def joined(band_part, column_part):
        return jnp.concatenate(
            [
                band_part.reshape(tokens_dev, half_width),
                column_part.reshape(tokens_dev, half_width),
            ],
            axis=1,
        )

    query_grad = joined(jnp.concatenate(query_band_grads, axis=0), row_grads[0])
    key_grad = joined(key_band_grad.astype(jnp.bfloat16), row_grads[1])
    value_grad = joined(value_band_grad.astype(jnp.bfloat16), row_grads[2])
    return (output, query_grad, key_grad, value_grad, proj_grad)


def solution(mesh):
    return jax.shard_map(
        local,
        mesh=mesh,
        in_specs=(
            P("seq", "head"),
            P("seq", "head"),
            P("seq", "head"),
            P("head", None),
            P("seq", "head"),
            P("seq"),
            P("seq"),
        ),
        out_specs=(
            P("seq", "head"),
            P("seq", "head"),
            P("seq", "head"),
            P("seq", "head"),
            P("head", "seq"),
        ),
        check_vma=False,
    )
```

profile of v0, /device:TPU:16, one launch (start us, length us, event | category | flops | bytes accessed | tf_op | source)
XLA Modules:
  0.0 952.6 jit_solution(4117811445177604135)
XLA Ops:
  10.4 16.1 %all-to-all-start = ((bf16[2,512,256]{2,0,1:T(2,128)(2,1)}), bf16[2,512,256]{2,0,1:T(2,128)(2,1)}, u32[]{:S(2)}, u32[]{:S(2)}) async-start(bf16[2,512,256]{2,0,1:T(2,128)(2,1)} %copy.161), calls=%async_computation | async-start | bytes 1048576 | tf_op jit(solution)/shard_map/all_to_all | solution.py:127
  28.4 2.0 collective-permute-start
  33.0 2.1 fusion.51
  36.9 27.3 %all-reduce.2 = s32[2048]{0:T(1024)S(1)} all-reduce(s32[2048]{0:T(1024)S(1)} %dynamic-update-slice.18), channel_id=1, replica_groups=mesh['seq'=128,'head'=2] {'seq'}, use_global_device_ids=true, to_apply=%add.2 | all-reduce | flops 2048 | bytes 16384
  70.9 2.4 copy.163
  73.3 15.0 %all-to-all-start.1 = ((bf16[2,512,256]{2,0,1:T(2,128)(2,1)}), bf16[2,512,256]{2,0,1:T(2,128)(2,1)}, u32[]{:S(2)}, u32[]{:S(2)}) async-start(bf16[2,512,256]{2,0,1:T(2,128)(2,1)} %copy.163), calls=%async_computation.1 | async-start | bytes 1048576 | tf_op jit(solution)/shard_map/all_to_all | solution.py:128
  93.5 6.6 convolution_convert_fusion.3
  100.1 5.8 all-to-all-done.1
  105.9 9.0 all-to-all-start.2
  118.8 4.9 fusion.3
  123.7 2.9 convolution_convert_fusion
  132.8 13.9 %all-to-all-start.4 = ((bf16[2,512,256]{2,0,1:T(2,128)(2,1)}), bf16[2,512,256]{2,0,1:T(2,128)(2,1)}, u32[]{:S(2)}, u32[]{:S(2)}) async-start(bf16[2,512,256]{2,0,1:T(2,128)(2,1)} %copy.178), calls=%async_computation.5 | async-start | bytes 1048576 | tf_op jit(solution)/shard_map/all_to_all | solution.py:214
  146.7 4.4 exponential_reduce_fusion.1
  160.0 2.2 copy.168
  162.3 2.8 reshape.895
  165.1 2.3 copy.170
  174.4 2.1 reshape.904
  178.2 2.7 copy.232
  180.8 4.7 multiply_reduce_fusion
  185.5 2.1 copy.171
  187.6 14.3 %all-to-all-start.3 = ((bf16[256,4,256]{2,1,0:T(4,128)(2,1)}), bf16[256,4,256]{2,1,0:T(4,128)(2,1)}, u32[]{:S(2)}, u32[]{:S(2)}) async-start(bf16[256,4,256]{2,1,0:T(4,128)(2,1)} %copy.171), calls=%async_computation.3 | async-start | bytes 1048576 | tf_op jit(solution)/shard_map/all_to_all | solution.py:146
  204.0 2.1 copy.151
  206.1 5.8 convolution_convert_fusion.4
  212.8 2.1 copy.173
  214.8 4.9 all-to-all-done.3
  223.7 4.5 fusion.18
  228.3 4.4 fusion.19
  235.7 5.5 multiply_convert_fusion.1
  241.2 2.0 copy-done.3
  247.2 5.8 convolution_bitcast_fusion.1
  256.9 4.5 collective-permute-start.1
  261.5 6.8 fusion.8
  269.1 3.5 convolution_convert_fusion.2
  273.7 8.7 all-to-all-start.7
  282.4 3.9 fusion.17
  289.4 2.1 copy.197
  291.5 8.8 all-to-all-done.7
  300.3 9.5 all-to-all-start.6
  309.9 8.6 multiply_convert_fusion
  319.7 2.1 copy.185
  321.8 5.9 all-to-all-done.6
  327.7 9.0 all-to-all-start.5
  336.7 3.1 fusion.16
  342.7 3.6 fusion.11
  356.8 2.2 pad_maximum_fusion.1
  361.1 450.0 %reduce-scatter.5.cloned.1.call-done = f32[512,8]{0,1:T(8,128)} async-done(((f32[512,1024]{0,1:T(8,128)}), f32[512,8]{0,1:T(8,128)}) %reduce-scatter.5.cloned.1.call-update) | async-done | bytes 16400 | tf_op jit(solution)/shard_map/reduce_scatter | solution.py:169
  812.4 130.5 %reduce-scatter.3.cloned.1.call-done = f32[1024,512]{1,0:T(8,128)} async-done(((f32[1024,1024]{1,0:T(8,128)}), f32[1024,512]{1,0:T(8,128)}) %reduce-scatter.3.cloned.1.call-update) | async-done | bytes 2097168 | tf_op jit(solution)/shard_map/reduce_scatter | solution.py:161
  942.9 2.7 convert_element_type.127
  (197 shorter events, 88.7 us)
Async XLA Ops:
  7.2 116.5 %copy-start = (bf16[512,1024]{1,0:T(8,128)(2,1)S(1)}, bf16[512,1024]{1,0:T(8,128)(2,1)}, u32[]{:S(2)}) copy-start(bf16[512,1024]{1,0:T(8,128)(2,1)} %param.22) | copy-start | bytes 3145732
  7.2 24.1 %copy-start.32 = (bf16[1024,512]{1,0:T(8,128)(2,1)S(1)}, bf16[1024,512]{1,0:T(8,128)(2,1)}, u32[]{:S(2)}) copy-start(bf16[1024,512]{1,0:T(8,128)(2,1)} %param.19) | copy-start | bytes 3145732
  7.2 19.4 %copy-start.29 = (bf16[1024,512]{1,0:T(8,128)(2,1)S(1)}, bf16[1024,512]{1,0:T(8,128)(2,1)}, u32[]{:S(2)}) copy-start(bf16[1024,512]{1,0:T(8,128)(2,1)} %param.20) | copy-start | bytes 3145732
  7.2 116.5 %all-gather.2.cloned.1.call-start = ((), (), s32[]{:S(2)}) async-start(), calls=%async_computation.11 | async-start | bytes 3145728 | tf_op jit(solution)/shard_map/all_gather | solution.py:164
  10.4 24.6 %copy-start.44 = (s32[16]{0:T(128)S(1)}, s32[16]{0:T(128)}, u32[]{:S(2)}) copy-start(s32[16]{0:T(128)} %param.24) | copy-start | bytes 196
  10.4 25.0 %copy-start.46 = (u32[256]{0:T(256)S(1)}, u32[256]{0:T(256)}, u32[]{:S(2)}) copy-start(u32[256]{0:T(256)} %constant.235) | copy-start | bytes 3076
  10.4 26.2 %copy-start.45 = (s32[16]{0:T(128)S(1)}, s32[16]{0:T(128)}, u32[]{:S(2)}) copy-start(s32[16]{0:T(128)} %param.25) | copy-start | bytes 196
  10.4 62.8 %all-to-all-start = ((bf16[2,512,256]{2,0,1:T(2,128)(2,1)}), bf16[2,512,256]{2,0,1:T(2,128)(2,1)}, u32[]{:S(2)}, u32[]{:S(2)}) async-start(bf16[2,512,256]{2,0,1:T(2,128)(2,1)} %copy.161), calls=%async_computation | async-start | bytes 1048576 | tf_op jit(solution)/shard_map/all_to_all | solution.py:127
  28.4 86.5 %collective-permute-start = (bf16[2,512,256]{2,1,0:T(8,128)(2,1)}, bf16[2,512,256]{2,1,0:T(8,128)(2,1)}, u32[]{:S(2)}, u32[]{:S(2)}) collective-permute-start(bf16[2,512,256]{2,1,0:T(8,128)(2,1)} %pad_maximum_fusion.8), channel_id=1, source_target_pairs={{0,2},{2,4},{4,6},{6,8},{8,10},{10,12},{12,14},{14,16},{16,18},{18... | collective-permute-start | bytes 1572872 | tf_op jit(solution)/shard_map/ppermute | solution.py:19
  32.1 32.3 %copy-start.38 = (bf16[512,256]{1,0:T(8,128)(2,1)S(1)}, bf16[512,256]{1,0:T(8,128)(2,1)}, u32[]{:S(2)}) copy-start(bf16[512,256]{1,0:T(8,128)(2,1)} %get-tuple-element.86) | copy-start | bytes 786436
  35.0 56.5 %copy-start.14 = (bf16[1024,256]{1,0:T(8,128)(2,1)}, bf16[1024,256]{1,0:T(8,128)(2,1)S(1)}, u32[]{:S(2)}) copy-start(bf16[1024,256]{1,0:T(8,128)(2,1)S(1)} %get-tuple-element.89) | copy-start | bytes 1572868
  65.8 195.6 %copy-start.10 = (pred[512,1024]{0,1:T(8,128)(4,1)}, pred[512,1024]{0,1:T(8,128)(4,1)S(1)}, u32[]{:S(2)}) copy-start(pred[512,1024]{0,1:T(8,128)(4,1)S(1)} %fusion.7) | copy-start | bytes 1572868
  67.5 3.4 copy-start.2
  68.6 21.7 %copy-start.26 = (bf16[1024,256]{1,0:T(8,128)(2,1)S(1)}, bf16[1024,256]{1,0:T(8,128)(2,1)}, u32[]{:S(2)}) copy-start(bf16[1024,256]{1,0:T(8,128)(2,1)} %get-tuple-element.90) | copy-start | bytes 1572868
  73.3 32.7 %all-to-all-start.1 = ((bf16[2,512,256]{2,0,1:T(2,128)(2,1)}), bf16[2,512,256]{2,0,1:T(2,128)(2,1)}, u32[]{:S(2)}, u32[]{:S(2)}) async-start(bf16[2,512,256]{2,0,1:T(2,128)(2,1)} %copy.163), calls=%async_computation.1 | async-start | bytes 1048576 | tf_op jit(solution)/shard_map/all_to_all | solution.py:128
  93.5 53.2 %copy-start.12 = (pred[512,1024]{0,1:T(8,128)(4,1)}, pred[512,1024]{0,1:T(8,128)(4,1)S(1)}, u32[]{:S(2)}) copy-start(pred[512,1024]{0,1:T(8,128)(4,1)S(1)} %fusion.6) | copy-start | bytes 1572868
  100.1 18.7 %copy-start.22 = (bf16[512,256]{0,1:T(8,128)(2,1)S(1)}, bf16[512,256]{0,1:T(8,128)(2,1)}, u32[]{:S(2)}) copy-start(bf16[512,256]{0,1:T(8,128)(2,1)} %copy.153) | copy-start | bytes 786436
  105.9 26.9 %all-to-all-start.2 = ((bf16[2,512,256]{2,0,1:T(2,128)(2,1)}), bf16[2,512,256]{2,0,1:T(2,128)(2,1)}, u32[]{:S(2)}, u32[]{:S(2)}) async-start(bf16[2,512,256]{2,0,1:T(2,128)(2,1)} %copy.167), calls=%async_computation.2 | async-start | bytes 1048576 | tf_op jit(solution)/shard_map/all_to_all | solution.py:129
  132.8 39.5 %all-to-all-start.4 = ((bf16[2,512,256]{2,0,1:T(2,128)(2,1)}), bf16[2,512,256]{2,0,1:T(2,128)(2,1)}, u32[]{:S(2)}, u32[]{:S(2)}) async-start(bf16[2,512,256]{2,0,1:T(2,128)(2,1)} %copy.178), calls=%async_computation.5 | async-start | bytes 1048576 | tf_op jit(solution)/shard_map/all_to_all | solution.py:214
  155.5 12.0 %copy-start.17 = (bf16[256,4,4,64]{0,3,2,1:T(8,128)(2,1)}, bf16[256,4,4,64]{0,3,2,1:T(8,128)(2,1)S(1)}, u32[]{:S(2)}) copy-start(bf16[256,4,4,64]{0,3,2,1:T(8,128)(2,1)S(1)} %copy.165) | copy-start | bytes 1572868
  160.0 9.3 copy-start.15
  167.5 3.9 copy-start.20
  187.6 32.1 %all-to-all-start.3 = ((bf16[256,4,256]{2,1,0:T(4,128)(2,1)}), bf16[256,4,256]{2,1,0:T(4,128)(2,1)}, u32[]{:S(2)}, u32[]{:S(2)}) async-start(bf16[256,4,256]{2,1,0:T(4,128)(2,1)} %copy.171), calls=%async_computation.3 | async-start | bytes 1048576 | tf_op jit(solution)/shard_map/all_to_all | solution.py:146
  201.9 609.2 %reduce-scatter.5.cloned.1.call-start = ((), (), s32[]{:S(2)}) async-start(), calls=%async_computation.12 | async-start | bytes 2113536 | tf_op jit(solution)/shard_map/reduce_scatter | solution.py:169
  206.1 5.8 copy-start.33
  228.3 714.7 %reduce-scatter.3.cloned.1.call-start = ((), (), s32[]{:S(2)}) async-start(), calls=%async_computation.10 | async-start | bytes 6291456 | tf_op jit(solution)/shard_map/reduce_scatter | solution.py:161
  235.6 5.5 copy-start.42
  235.7 7.6 copy-start.23
  244.6 8.4 copy-start.8
  256.9 90.9 %collective-permute-start.1 = (bf16[2,512,256]{2,1,0:T(8,128)(2,1)}, bf16[2,512,256]{2,1,0:T(8,128)(2,1)}, u32[]{:S(2)}, u32[]{:S(2)}) collective-permute-start(bf16[2,512,256]{2,1,0:T(8,128)(2,1)} %pad_maximum_fusion.11), channel_id=1, source_target_pairs={{2,0},{4,2},{6,4},{8,6},{10,8},{12,10},{14,12},{16,14},{18,16},{20... | collective-permute-start | bytes 1572872 | tf_op jit(solution)/shard_map/ppermute | solution.py:19
  261.5 7.6 copy-start.21
  269.1 4.6 copy-start.40
  273.7 26.7 %all-to-all-start.7 = ((bf16[256,4,256]{2,1,0:T(4,128)(2,1)}), bf16[256,4,256]{2,1,0:T(4,128)(2,1)}, u32[]{:S(2)}, u32[]{:S(2)}) async-start(bf16[256,4,256]{2,1,0:T(4,128)(2,1)} %copy.204), calls=%async_computation.8 | async-start | bytes 1048576 | tf_op jit(solution)/shard_map/all_to_all | solution.py:240
  282.4 3.9 copy-start.5
  282.4 3.9 copy-start.39
  282.4 3.9 copy-start.41
  287.8 22.0 %copy-start.11 = (pred[512,1024]{0,1:T(8,128)(4,1)S(1)}, pred[512,1024]{0,1:T(8,128)(4,1)}, u32[]{:S(2)}) copy-start(pred[512,1024]{0,1:T(8,128)(4,1)} %copy-done.10) | copy-start | bytes 1572868
  300.3 27.3 %all-to-all-start.6 = ((bf16[256,4,256]{2,1,0:T(4,128)(2,1)}), bf16[256,4,256]{2,1,0:T(4,128)(2,1)}, u32[]{:S(2)}, u32[]{:S(2)}) async-start(bf16[256,4,256]{2,1,0:T(4,128)(2,1)} %copy.197), calls=%async_computation.7 | async-start | bytes 1048576 | tf_op jit(solution)/shard_map/all_to_all | solution.py:233
  309.8 8.6 copy-start.16
  318.4 18.2 %copy-start.7 = (bf16[1024,256]{0,1:T(8,128)(2,1)S(1)}, bf16[1024,256]{0,1:T(8,128)(2,1)}, u32[]{:S(2)}) copy-start(bf16[1024,256]{0,1:T(8,128)(2,1)} %copy-done.6) | copy-start | bytes 1572868
  321.8 18.0 %copy-start.35 = (bf16[512,1,4,64]{0,3,2,1:T(8,128)(2,1)S(1)}, bf16[512,1,4,64]{0,3,2,1:T(8,128)(2,1)}, u32[]{:S(2)}) copy-start(bf16[512,1,4,64]{0,3,2,1:T(8,128)(2,1)} %fusion.17) | copy-start | bytes 786436
  327.7 27.0 %all-to-all-start.5 = ((bf16[256,4,256]{2,1,0:T(4,128)(2,1)}), bf16[256,4,256]{2,1,0:T(4,128)(2,1)}, u32[]{:S(2)}, u32[]{:S(2)}) async-start(bf16[256,4,256]{2,1,0:T(4,128)(2,1)} %copy.185), calls=%async_computation.6 | async-start | bytes 1048576 | tf_op jit(solution)/shard_map/all_to_all | solution.py:226
  336.7 4.2 copy-start.19
  339.8 2.9 copy-start.9
  342.7 4.9 copy-start.25
  349.0 7.8 copy-start.27
  356.8 3.3 copy-start.28
  356.8 588.8 %copy-start.1 = (bf16[512,1024]{1,0:T(8,128)(2,1)S(1)}, bf16[512,1024]{1,0:T(8,128)(2,1)}, u32[]{:S(2)}) copy-start(bf16[512,1024]{1,0:T(8,128)(2,1)} %param.22) | copy-start | bytes 3145732
  (12 other events, 20.3 us)
Sparse Core Ops, SparseCore 0:
  9.8 51.9 all-gather.1
  228.4 582.6 reduce-scatter.4
  813.8 129.0 reduce-scatter.2
where the time goes:
time: 963 us; the launch traced here: 953 us
  waiting for transfers between devices  609 us (63%)
  starting transfers between devices  102 us (11%)
  matrix products  83.7 us (9%)
  local copies, waits for them, and re-layouts  83.5 us (9%)
  other arithmetic  31.5 us (3%)
  blocking collectives  27.3 us (3%)
  between operations  15.7 us (2%)
    reduce_scatter x1, waiting for transfers between devices, local(): lax.psum_scatter(proj_term, 'seq', scatter_dimension=1, tiled=True)  450 us
    reduce_scatter x1, waiting for transfers between devices, local(): lax.psum_scatter(partial_out, 'head', scatter_dimension=1, tiled=True)  131 us
    unnamed x1, blocking collectives  27.3 us
  transfers between devices with their start and end apart: 13, of which 8 were waited for; matrix products, arithmetic and copies ran while one was open for 17% of the time, Pallas kernels for 0%

commit v1 on v0

v1 whole, which is shorter than its diff:
```python
import functools
import math

import jax
import jax.numpy as jnp
from jax import lax
from jax.experimental import pallas as pl
from jax.experimental.pallas import tpu as pltpu
from jax.sharding import PartitionSpec as P

HEAD_DIM = 64
STRIDE = 512
BLOCK = 64
TILE = 256
MASKED = -1e30
F32 = jnp.float32
BF16 = jnp.bfloat16


def dot(a, b):
    return jnp.dot(a, b, preferred_element_type=F32)


def pair_tile(q, k, v, d, allowed):
    nq = q.shape[0]
    qs = (q.astype(F32) * HEAD_DIM**-0.5).astype(BF16)
    q_t, d_t, k_t, v_t = (m.astype(F32).T.astype(BF16) for m in (qs, d, k, v))
    low = lax.broadcasted_iota(jnp.int32, (nq, 2 * HEAD_DIM), 1) < HEAD_DIM
    blank = jnp.zeros((HEAD_DIM, nq), BF16)
    nothing = jnp.zeros_like(q)
    outs, dqs, dk, dv = [], [], None, None
    for h in range(2):
        mine = slice(h * HEAD_DIM, (h + 1) * HEAD_DIM)

        def alone(m_t):
            return jnp.concatenate([m_t[mine], blank] if h == 0 else [blank, m_t[mine]], axis=0)

        scores = jnp.where(allowed, dot(k, alone(q_t)), MASKED)
        highest = jnp.max(scores, axis=0, keepdims=True)
        weights = jnp.exp(scores - highest)
        weights = weights * (1.0 / jnp.sum(weights, axis=0, keepdims=True))
        low_weights = weights.astype(BF16)
        out_t = dot(v_t[mine], low_weights).astype(BF16).astype(F32)
        delta = jnp.sum(out_t * d_t[mine].astype(F32), axis=0, keepdims=True)
        d_scores = (weights * (dot(v, alone(d_t)) - delta)).astype(BF16)
        outs.append(out_t)
        dqs.append(dot(k_t[mine], d_scores) * HEAD_DIM**-0.5)
        keep = low if h == 0 else jnp.logical_not(low)
        dk_h = dot(d_scores, jnp.where(keep, qs, nothing))
        dv_h = dot(low_weights, jnp.where(keep, d, nothing))
        dk = dk_h if dk is None else dk + dk_h
        dv = dv_h if dv is None else dv + dv_h
    return jnp.concatenate(outs, axis=0).T, jnp.concatenate(dqs, axis=0).T, dk, dv


def band_kernel(q_ref, k_ref, v_ref, d_ref, low_ref, out_ref, dq_ref, dk_ref, dv_ref, dk_sum, dv_sum):
    tokens, width = q_ref.shape
    span = TILE + STRIDE
    for pair in range(width // 128):
        lanes = slice(pair * 128, pair * 128 + 128)
        dk_sum[...] = jnp.zeros_like(dk_sum)
        dv_sum[...] = jnp.zeros_like(dv_sum)

        @pl.loop(0, tokens // TILE)
        def _(step):
            begin = pl.multiple_of(step * TILE, TILE)
            mine, reach = pl.ds(begin, TILE), pl.ds(begin, span)
            key_at = begin + lax.broadcasted_iota(jnp.int32, (span, TILE), 0)
            query_at = STRIDE + begin + lax.broadcasted_iota(jnp.int32, (span, TILE), 1)
            allowed = (key_at <= query_at) & (key_at >= low_ref[:, mine])
            out, dq, dk, dv = pair_tile(
                q_ref[mine, lanes], k_ref[reach, lanes], v_ref[reach, lanes], d_ref[mine, lanes], allowed
            )
            out_ref[mine, lanes] = out.astype(BF16)
            dq_ref[mine, lanes] = dq.astype(BF16)
            dk_sum[reach, :] += dk
            dv_sum[reach, :] += dv

        dk_ref[:, lanes] = dk_sum[...]
        dv_ref[:, lanes] = dv_sum[...]


def column_kernel(qkv_ref, d_ref, reach_ref, res_ref, wide, back):
    devices = qkv_ref.shape[0]
    rows = 2 * devices
    flat = devices * 16
    for t in range(3):
        wide[t] = qkv_ref[:, pl.ds(16 * t, 16), :].astype(F32).reshape(flat, 128)
    wide[3] = d_ref[...].astype(F32).reshape(flat, 128)
    key_at = lax.broadcasted_iota(jnp.int32, (rows, rows), 0)
    query_at = lax.broadcasted_iota(jnp.int32, (rows, rows), 1)

    @pl.loop(0, 8)
    def _(column):
        at = pl.ds(column, rows, stride=8)
        allowed = (key_at <= query_at) & (query_at - key_at < reach_ref[...])
        q, k, v, d = (wide[t, at, :].astype(BF16) for t in range(4))
        for t, value in enumerate(pair_tile(q, k, v, d, allowed)):
            back[t, at, :] = value

    for t in range(4):
        res_ref[:, pl.ds(16 * t, 16), :] = back[t].reshape(devices, 16, 128).astype(BF16)


def vmem(n):
    return [pl.BlockSpec(memory_space=pltpu.VMEM)] * n


def swap_head(x):
    return lax.ppermute(x, "head", [(0, 1), (1, 0)])


def to_messages(matrix, half):
    rows = matrix.shape[0] // STRIDE
    grid = matrix[:, half:].reshape(rows, STRIDE // 8, 8, half // 128, 128)
    return grid.transpose(1, 3, 0, 2, 4).reshape(STRIDE // 8 * (half // 128), rows * 8, 128)


def from_messages(messages, half):
    rows = messages.shape[1] // 8
    grid = messages.reshape(STRIDE // 8, half // 128, rows, 8, 128)
    return grid.transpose(2, 0, 3, 1, 4).reshape(rows * STRIDE, half)


def local(queries, key_rows, value_rows, out_proj, grad_out, band_blocks, column_reach):
    tokens, width = queries.shape
    half = width // 2
    seq_devices = lax.axis_size("seq")
    me = lax.axis_index("seq")
    head = lax.axis_index("head")

    reach = column_reach.reshape(2, STRIDE // BLOCK).T.astype(BF16)
    reach = jnp.repeat(reach, seq_devices // (STRIDE // BLOCK), axis=0)
    reach = jnp.pad(reach[:, None, :], ((0, 0), (0, 7), (0, 126)))
    qkv = jnp.concatenate([to_messages(m, half) for m in (queries, key_rows, value_rows)] + [reach], axis=1)
    qkv = lax.all_to_all(qkv, "seq", 0, 0, tiled=True)
    reach_rows = qkv[:, 48, :2].reshape(1, 2 * seq_devices).astype(jnp.int32)

    grad_other = swap_head(grad_out)
    first = jnp.where(head == 0, grad_out, grad_other)
    second = jnp.where(head == 0, grad_other, grad_out)
    grad_all = jnp.concatenate([first, second], axis=1)
    other_half = lax.dynamic_slice_in_dim(out_proj, (1 - head) * width, width, 1)
    proj_other = swap_head(other_half)
    proj_mine = lax.dynamic_slice_in_dim(out_proj, head * width, width, 1)
    d_attended = lax.dot_general(
        grad_all, out_proj, (((1,), (1,)), ((), ())), preferred_element_type=F32
    ).astype(BF16)
    d_column = lax.all_to_all(to_messages(d_attended, half), "seq", 0, 0, tiled=True)

    rim = jnp.stack([m[tokens - STRIDE :, :half] for m in (key_rows, value_rows)])
    rim = lax.ppermute(rim, "seq", [(i, i + 1) for i in range(seq_devices - 1)])
    key_ext = jnp.concatenate([rim[0], key_rows[:, :half]], axis=0)
    value_ext = jnp.concatenate([rim[1], value_rows[:, :half]], axis=0)
    block_at = jnp.arange(tokens // BLOCK, dtype=jnp.int32)
    lowest = (block_at + STRIDE // BLOCK - band_blocks + 1) * BLOCK
    lowest = jnp.maximum(lowest, jnp.where(me == 0, STRIDE, 0))
    lowest = jnp.repeat(lowest, BLOCK)[None, :]
    flops = 6 * 2 * tokens * (TILE + STRIDE) * half
    band_out, band_dq, band_dk, band_dv = pl.pallas_call(
        band_kernel,
        out_shape=(
            jax.ShapeDtypeStruct((tokens, half), BF16),
            jax.ShapeDtypeStruct((tokens, half), BF16),
            jax.ShapeDtypeStruct((tokens + STRIDE, half), F32),
            jax.ShapeDtypeStruct((tokens + STRIDE, half), F32),
        ),
        in_specs=vmem(5),
        out_specs=tuple(vmem(4)),
        scratch_shapes=[pltpu.VMEM((tokens + STRIDE, 128), F32)] * 2,
        compiler_params=pltpu.CompilerParams(vmem_limit_bytes=40 * 2**20),
        cost_estimate=pl.CostEstimate(flops=4 * flops, bytes_accessed=8 * 2**20, transcendentals=0),
    )(queries[:, :half], key_ext, value_ext, d_attended[:, :half], lowest)
    rim_back = jnp.stack([band_dk[:STRIDE], band_dv[:STRIDE]]).astype(BF16)
    rim_back = lax.ppermute(rim_back, "seq", [(i + 1, i) for i in range(seq_devices - 1)]).astype(F32)

    column_results = pl.pallas_call(
        column_kernel,
        out_shape=jax.ShapeDtypeStruct((seq_devices, 64, 128), BF16),
        in_specs=vmem(3),
        out_specs=vmem(1)[0],
        scratch_shapes=[pltpu.VMEM((4, seq_devices * 16, 128), F32)] * 2,
        compiler_params=pltpu.CompilerParams(vmem_limit_bytes=48 * 2**20),
        cost_estimate=pl.CostEstimate(flops=flops, bytes_accessed=8 * 2**20, transcendentals=0),
    )(qkv, d_column, reach_rows)
    out_back = lax.all_to_all(column_results[:, :16], "seq", 0, 0, tiled=True)
    grads_back = lax.all_to_all(column_results[:, 16:], "seq", 0, 0, tiled=True)

    attended = jnp.concatenate([band_out, from_messages(out_back, half)], axis=1)
    attended_other = swap_head(attended)
    output = (dot(attended, proj_mine) + dot(attended_other, proj_other)).astype(BF16)

    term = lax.dot_general(grad_all, attended, (((0,), (0,)), ((), ())), preferred_element_type=F32)
    parts = term.reshape(4, 8, 2, 2, 8 * width)
    core = lax.rem(me, 2)
    x_hi = lax.rem(me // 2, 2)

    def halve(parts, bit, distance):
        keep = jnp.where(bit == 0, parts[:, :, 0], parts[:, :, 1])
        send = jnp.where(bit == 0, parts[:, :, 1], parts[:, :, 0])
        return keep + lax.ppermute(send, "seq", [(i, i ^ distance) for i in range(seq_devices)])

    parts = halve(parts.transpose(0, 1, 3, 2, 4), core, 1)
    parts = halve(parts, x_hi, 2)
    y_groups = [[y * 32 + rest for y in range(4)] for rest in range(32)]
    z_groups = [[y * 32 + z * 4 + rest for z in range(8)] for y in range(4) for rest in range(4)]
    parts = lax.all_to_all(parts, "seq", 0, 0, axis_index_groups=y_groups, tiled=True).sum(0)
    parts = lax.all_to_all(parts, "seq", 0, 0, axis_index_groups=z_groups, tiled=True).sum(0)
    proj_grad = parts.reshape(8, width).T * (1.0 / math.sqrt(tokens * seq_devices))

    grads = from_messages(grads_back[:, :16], half), from_messages(grads_back[:, 16:32], half), from_messages(grads_back[:, 32:], half)
    query_grad = jnp.concatenate([band_dq, grads[0]], axis=1)

    def joined(ext, rim, column):
        last = (ext[tokens:] + rim).astype(BF16)
        band = jnp.concatenate([ext[STRIDE:tokens].astype(BF16), last], axis=0)
        return jnp.concatenate([band, column], axis=1)

    return (
        output,
        query_grad,
        joined(band_dk, rim_back[0], grads[1]),
        joined(band_dv, rim_back[1], grads[2]),
        proj_grad,
    )


def solution(mesh):
    tokens = P("seq", "head")
    return jax.shard_map(
        local,
        mesh=mesh,
        in_specs=(tokens, tokens, tokens, P("head", None), tokens, P("seq"), P("seq")),
        out_specs=(tokens, tokens, tokens, tokens, P("head", "seq")),
        check_vma=False,
    )
```

time: 963 us -> 310 us (0.32)
  waiting for transfers between devices: 609 us -> 118 us
  matrix products: 83.7 us -> 9.17 us
  local copies, waits for them, and re-layouts: 83.5 us -> 33.9 us
  Pallas kernels: 0 us -> 35.1 us
  blocking collectives: 27.3 us -> 0 us
  starting transfers between devices: 102 us -> 82.7 us
  between operations: 15.7 us -> 1.05 us
    reduce_scatter x2 -> x0, waiting for transfers between devices: 580 us -> none  [the longest x1 450 us: local(): lax.psum_scatter(proj_term, 'seq', scatter_dimension=1, tiled=True)]
    ppermute x2 -> x7, waiting for transfers between devices: 0.01 us -> 95.7 us  [the longest x3 55 us: swap_head(): return lax.ppermute(x, 'head', [(0, 1), (1, 0)])]
    dot_general x21 -> x4, matrix products: 83.7 us -> 9.17 us  [the longest x1 4.15 us: local(): lax.dot_general(grad_all, attended, (((0,), (0,)), ((), ())), preferred_e...]
    pallas_call x0 -> x2, Pallas kernels: none -> 35.1 us  [the longest x1 21.7 us: local(): pl.pallas_call(band_kernel, out_shape=(jax.ShapeDtypeStruct((tokens, half...]
    reshape x25 -> x5, local copies, waits for them, and re-layouts: 38.4 us -> 5.17 us  [the longest x1 4.01 us: local(): parts = term.reshape(4, 8, 2, 2, 8 * width)]
    unnamed x1 -> x0, blocking collectives: 27.3 us -> none
    all_to_all x8 -> x6, starting transfers between devices: 95.5 us -> 69 us  [the longest x1 19.3 us: local(): lax.all_to_all(to_messages(d_attended, half), 'seq', 0, 0, tiled=True)]
    all_to_all x8 -> x1, local copies, waits for them, and re-layouts: 12.6 us -> 0.75 us  [local(): lax.all_to_all(parts, 'seq', 0, 0, axis_index_groups=z_groups, tiled=True)]
  transfers between devices with their start and end apart: 13 -> 13, of which waited for: 8 -> 8; matrix products, arithmetic and copies ran while one was open for 17% -> 10% of each run, Pallas kernels for 0% -> 7%
where the time goes in v1:
time: 310 us; the launch traced here: 308 us
  waiting for transfers between devices  118 us (38%)
  starting transfers between devices  82.7 us (27%)
  Pallas kernels  35.1 us (11%)
  local copies, waits for them, and re-layouts  33.9 us (11%)
  other arithmetic  28.3 us (9%)
  matrix products  9.17 us (3%)
    ppermute x3, waiting for transfers between devices, swap_head(): return lax.ppermute(x, 'head', [(0, 1), (1, 0)])  55 us
    ppermute x1, waiting for transfers between devices, local(): lax.ppermute(rim_back, 'seq', [(i + 1, i) for i in range(seq_devices - 1)])  25.3 us
    pallas_call x1, Pallas kernels, local(): pl.pallas_call(band_kernel, out_shape=(jax.ShapeDtypeStruct((tokens, half...  21.7 us
    all_to_all x1, starting transfers between devices, local(): lax.all_to_all(to_messages(d_attended, half), 'seq', 0, 0, tiled=True)  19.3 us
    all_to_all x1, starting transfers between devices, local(): qkv = lax.all_to_all(qkv, 'seq', 0, 0, tiled=True)  15.9 us
    ppermute x2, waiting for transfers between devices, halve(): lax.ppermute(send, 'seq', [(i, i ^ distance) for i in range(seq_devices)])  15.3 us
    all_to_all x1, waiting for transfers between devices, local(): lax.all_to_all(to_messages(d_attended, half), 'seq', 0, 0, tiled=True)  14.7 us
    all_to_all x1, starting transfers between devices, local(): grads_back = lax.all_to_all(column_results[:, 16:], 'seq', 0, 0, tiled=True)  14.4 us
  transfers between devices with their start and end apart: 13, of which 8 were waited for; matrix products, arithmetic and copies ran while one was open for 10% of the time, Pallas kernels for 7%

profile of v1, /device:TPU:16, one launch (start us, length us, event | category | flops | bytes accessed | tf_op | source)
XLA Modules:
  0.0 308.4 jit_solution(17287529872977642199)
XLA Ops:
  1.8 2.1 fusion.23
  5.3 1.5 fusion.1
  6.8 15.9 %all-to-all-start = ((bf16[128,56,128]{2,1,0:T(8,128)(2,1)}), bf16[128,56,128]{2,1,0:T(8,128)(2,1)}, u32[]{:S(2)}, u32[]{:S(2)}) async-start(bf16[128,56,128]{2,1,0:T(8,128)(2,1)} %fusion.1), calls=%async_computation | async-start | bytes 3670016 | tf_op jit(solution)/shard_map/all_to_all | solution.py:136
  23.5 1.1 slice_bitcast_fusion.6
  25.4 1.9 collective-permute-start
  27.3 38.9 %collective-permute-done.1 = bf16[1024,512]{1,0:T(8,128)(2,1)} collective-permute-done((bf16[1024,512]{1,0:T(8,128)(2,1)}, bf16[1024,512]{1,0:T(8,128)(2,1)}, u32[]{:S(2)}, u32[]{:S(2)}) %collective-permute-start.1) | collective-permute-done | bytes 1048608 | tf_op jit(solution)/shard_map/ppermute | solution.py:110
  66.2 1.7 broadcast_select_fusion.3
  68.0 1.3 convolution_convert_fusion
  71.0 19.3 %all-to-all-start.1 = ((bf16[128,16,128]{2,1,0:T(8,128)(2,1)}), bf16[128,16,128]{2,1,0:T(8,128)(2,1)S(1)}, u32[]{:S(2)}, u32[]{:S(2)}) async-start(bf16[128,16,128]{2,1,0:T(8,128)(2,1)} %bitcast.82), calls=%async_computation.1 | async-start | bytes 1048576 | tf_op jit(solution)/shard_map/all_to_all | solution.py:149
  90.6 1.1 slice_bitcast_fusion.4
  92.6 1.2 fusion.13
  93.9 14.7 %all-to-all-done.1.d_ref = bf16[128,16,128]{2,1,0:T(8,128)(2,1)S(1)} async-done(((bf16[128,16,128]{2,1,0:T(8,128)(2,1)}), bf16[128,16,128]{2,1,0:T(8,128)(2,1)S(1)}, u32[]{:S(2)}, u32[]{:S(2)}) %all-to-all-start.1) | async-done | bytes 524320 | tf_op jit(solution)/shard_map/all_to_all | solution.py:149
  108.6 13.4 %shard_map.111 = bf16[128,64,128]{2,1,0:T(8,128)(2,1)S(1)} custom-call(bf16[128,56,128]{2,1,0:T(8,128)(2,1)} %all-to-all-done.qkv_ref, bf16[128,16,128]{2,1,0:T(8,128)(2,1)S(1)} %all-to-all-done.1.d_ref, s32[1,256]{1,0:T(1,128)S(1)} %reshape.107.reach_ref), custom_call_target="tpu_custom_call" | custom-call | flops 2415919104 | bytes 8388608 | tf_op jit(solution)/shard_map/pallas_call | solution.py:177
  122.0 1.4 copy-done.3
  124.2 9.1 %all-to-all-start.2 = ((bf16[128,16,128]{2,1,0:T(8,128)(2,1)}), bf16[128,16,128]{2,1,0:T(8,128)(2,1)}, u32[]{:S(2)}, u32[]{:S(2)}) async-start(bf16[128,16,128]{2,1,0:T(8,128)(2,1)} %slice.133), calls=%async_computation.2 | async-start | bytes 1048576 | tf_op jit(solution)/shard_map/all_to_all | solution.py:186
  133.3 1.1 copy-done.4
  136.5 21.7 %shard_map.110 = (bf16[1024,256]{1,0:T(8,128)(2,1)S(1)}, bf16[1024,256]{1,0:T(8,128)(2,1)S(1)}, f32[1536,256]{1,0:T(8,128)S(1)}, f32[1536,256]{1,0:T(8,128)S(1)}) custom-call(bf16[1024,256]{1,0:T(8,128)(2,1)S(1)} %copy-done.7, bf16[1536,256]{1,0:T(8,128)(2,1)S(1)} %copy-done.4, bf16[1536,256]{1,0:T(8,128)(2,1)S(1)} %pad_maximum_fusion.8.v_ref, ...), custom_call_target="tpu_custom_call" | custom-call | flops 9663676416 | bytes 8388608 | tf_op jit(solution)/shard_map/pallas_call | solution.py:160
  158.2 1.2 copy-done.1
  160.2 1.1 copy.51
  162.2 4.1 %fusion.2 = f32[1024,512]{1,0:T(8,128)} fusion(bf16[1024,512]{1,0:T(8,128)(2,1)} %copy-done.15, bf16[1024,512]{1,0:T(8,128)(2,1)} %copy-done.14, bf16[1024,256]{1,0:T(8,128)(2,1)S(1)} %bitcast.79, bf16[1024,256]{1,0:T(8,128)(2,1)S(1)} %get-tuple-element.9), kind=kOutput, calls=%fused_computation.7 | convolution fusion | flops 1080033280 | bytes 5242880 | tf_op jit(solution)/shard_map/dot_general | solution.py:193
  166.3 4.0 %reshape.106 = f32[4,8,2,2,4096]{4,3,2,1,0:T(2,128)} reshape(f32[1024,512]{1,0:T(8,128)} %fusion.2) | data formatting | bytes 4194304 | tf_op jit(solution)/shard_map/reshape | solution.py:194
  170.3 5.4 %fusion.17 = (f32[4,8,1,2,4096]{4,2,3,1,0:T(1,128)}, f32[4,8,1,2,4096]{4,2,3,1,0:T(1,128)S(1)}, f32[4,8,1,2,4096]{4,2,3,1,0:T(1,128)}) fusion(f32[4,8,2,2,4096]{4,2,3,1,0:T(2,128)} %bitcast.78, pred[]{:T(512)S(6)} %eq.18), kind=kLoop, calls=%fused_computation.49 | loop fusion | flops 262144 | bytes 5242881 | tf_op jit(solution)/shard_map/slice | solution.py:199
  175.7 1.8 copy.81
  177.7 2.8 collective-permute-done.5
  180.5 3.8 %fusion.4 = f32[4,8,2,4096]{3,2,1,0:T(2,128)S(1)} fusion(f32[4,8,2,4096]{3,2,1,0:T(2,128)} %collective-permute-done.5, f32[4,8,1,2,4096]{4,2,3,1,0:T(1,128)} %get-tuple-element.15, f32[4,8,1,2,4096]{4,2,3,1,0:T(1,128)} %get-tuple-element.13, pred[]{:T(512)S(6)} %eq.18), kind=kLoop, calls=%fused_computation.14 | loop fusion | flops 524288 | bytes 4194305 | tf_op jit(solution)/shard_map/add | solution.py:201
  184.3 1.3 fusion.19
  186.0 3.1 collective-permute-start.6
  189.0 12.5 %collective-permute-done.6 = f32[4,8,4096]{2,1,0:T(8,128)S(1)} collective-permute-done((f32[4,8,4096]{2,1,0:T(8,128)S(1)}, f32[4,8,4096]{2,1,0:T(8,128)S(1)}, u32[]{:S(2)}, u32[]{:S(2)}) %collective-permute-start.6) | collective-permute-done | bytes 524320 | tf_op jit(solution)/shard_map/ppermute | solution.py:201
  201.5 1.5 fusion.10
  203.0 4.9 %all-to-all-start.4 = ((f32[4,8,4096]{2,1,0:T(8,128)}), f32[4,8,4096]{2,1,0:T(8,128)}, u32[]{:S(2)}, u32[]{:S(2)}) async-start(f32[4,8,4096]{2,1,0:T(8,128)} %fusion.10), calls=%async_computation.4 | async-start | bytes 1048576 | tf_op jit(solution)/shard_map/all_to_all | solution.py:207
  207.9 2.7 slice.134
  210.6 3.7 %all-to-all-done.4 = f32[4,8,4096]{2,1,0:T(8,128)} async-done(((f32[4,8,4096]{2,1,0:T(8,128)}), f32[4,8,4096]{2,1,0:T(8,128)}, u32[]{:S(2)}, u32[]{:S(2)}) %all-to-all-start.4) | async-done | bytes 524320 | tf_op jit(solution)/shard_map/all_to_all | solution.py:207
  214.3 14.4 %all-to-all-start.3 = ((bf16[128,48,128]{2,1,0:T(8,128)(2,1)}), bf16[128,48,128]{2,1,0:T(8,128)(2,1)}, u32[]{:S(2)}, u32[]{:S(2)}) async-start(bf16[128,48,128]{2,1,0:T(8,128)(2,1)} %slice.134), calls=%async_computation.3 | async-start | bytes 3145728 | tf_op jit(solution)/shard_map/all_to_all | solution.py:187
  228.8 1.3 copy-done.2
  231.7 1.1 pad_maximum_fusion.3
  233.8 7.0 %collective-permute-start.4 = (bf16[2,512,256]{2,1,0:T(8,128)(2,1)}, bf16[2,512,256]{2,1,0:T(8,128)(2,1)}, u32[]{:S(2)}, u32[]{:S(2)}) collective-permute-start(bf16[2,512,256]{2,1,0:T(8,128)(2,1)} %pad_maximum_fusion.10), channel_id=1, source_target_pairs={{2,0},{4,2},{6,4},{8,6},{10,8},{12,10},{14,12},{16,14},{18,16},{20... | collective-permute-start | bytes 1572872 | tf_op jit(solution)/shard_map/ppermute | solution.py:175
  242.3 25.3 %collective-permute-done.4 = bf16[2,512,256]{2,1,0:T(8,128)(2,1)} collective-permute-done((bf16[2,512,256]{2,1,0:T(8,128)(2,1)}, bf16[2,512,256]{2,1,0:T(8,128)(2,1)}, u32[]{:S(2)}, u32[]{:S(2)}) %collective-permute-start.4) | collective-permute-done | bytes 524320 | tf_op jit(solution)/shard_map/ppermute | solution.py:175
  267.6 1.1 convert_element_type.41
  268.7 1.9 fusion.6
  271.3 16.1 %collective-permute-done.3 = bf16[512,512]{1,0:T(8,128)(2,1)} collective-permute-done((bf16[512,512]{1,0:T(8,128)(2,1)}, bf16[512,512]{1,0:T(8,128)(2,1)}, u32[]{:S(2)}, u32[]{:S(2)}) %collective-permute-start.3) | collective-permute-done | bytes 524320 | tf_op jit(solution)/shard_map/ppermute | solution.py:110
  287.4 3.0 add_convert_fusion
  290.5 1.1 reduce_sum.18
  292.3 5.3 %all-to-all-start.5 = ((f32[8,1,4096]{2,1,0:T(1,128)}), f32[8,1,4096]{2,1,0:T(1,128)S(1)}, u32[]{:S(2)}, u32[]{:S(2)}) async-start(f32[8,1,4096]{2,1,0:T(1,128)} %all_to_all.26), calls=%async_computation.5 | async-start | bytes 262144 | tf_op jit(solution)/shard_map/all_to_all | solution.py:208
  297.6 1.7 fusion.18
  300.3 1.1 pad_maximum_fusion.4
  301.4 1.1 pad_maximum_fusion.6
  302.4 1.1 pad_maximum_fusion.5
  303.5 4.2 %all-to-all-done.5 = f32[8,1,4096]{2,1,0:T(1,128)S(1)} async-done(((f32[8,1,4096]{2,1,0:T(1,128)}), f32[8,1,4096]{2,1,0:T(1,128)S(1)}, u32[]{:S(2)}, u32[]{:S(2)}) %all-to-all-start.5) | async-done | bytes 131104 | tf_op jit(solution)/shard_map/all_to_all | solution.py:208
  (80 shorter events, 19.4 us)
Async XLA Ops:
  0.6 67.3 %copy-start = (bf16[512,1024]{1,0:T(8,128)(2,1)S(1)}, bf16[512,1024]{1,0:T(8,128)(2,1)}, u32[]{:S(2)}) copy-start(bf16[512,1024]{1,0:T(8,128)(2,1)} %param.10) | copy-start | bytes 3145732
  1.8 2.3 copy-start.13
  4.0 1.2 copy-start.12
  6.8 64.2 %all-to-all-start = ((bf16[128,56,128]{2,1,0:T(8,128)(2,1)}), bf16[128,56,128]{2,1,0:T(8,128)(2,1)}, u32[]{:S(2)}, u32[]{:S(2)}) async-start(bf16[128,56,128]{2,1,0:T(8,128)(2,1)} %fusion.1), calls=%async_computation | async-start | bytes 3670016 | tf_op jit(solution)/shard_map/all_to_all | solution.py:136
  22.8 43.5 %collective-permute-start.1 = (bf16[1024,512]{1,0:T(8,128)(2,1)}, bf16[1024,512]{1,0:T(8,128)(2,1)}, u32[]{:S(2)}, u32[]{:S(2)}) collective-permute-start(bf16[1024,512]{1,0:T(8,128)(2,1)} %param.11), channel_id=1, source_target_pairs={{0,1},{1,0},{2,3},{3,2},{4,5},{5,4},{6,7},{7,6},{8,9},{9,8},{10,11... | collective-permute-start | bytes 3145736 | tf_op jit(solution)/shard_map/ppermute | solution.py:110
  25.4 65.2 %collective-permute-start = (bf16[2,512,256]{2,1,0:T(8,128)(2,1)}, bf16[2,512,256]{2,1,0:T(8,128)(2,1)}, u32[]{:S(2)}, u32[]{:S(2)}) collective-permute-start(bf16[2,512,256]{2,1,0:T(8,128)(2,1)} %pad_maximum_fusion.9), channel_id=1, source_target_pairs={{0,2},{2,4},{4,6},{6,8},{8,10},{10,12},{12,14},{14,16},{16,18},{18... | collective-permute-start | bytes 1572872 | tf_op jit(solution)/shard_map/ppermute | solution.py:152
  67.9 1.3 copy-start.14
  67.9 1.3 copy-start.15
  69.3 21.1 %copy-start.19 = (s32[16]{0:T(128)S(1)}, s32[16]{0:T(128)}, u32[]{:S(2)}) copy-start(s32[16]{0:T(128)} %param.12) | copy-start | bytes 196
  71.0 37.5 %all-to-all-start.1 = ((bf16[128,16,128]{2,1,0:T(8,128)(2,1)}), bf16[128,16,128]{2,1,0:T(8,128)(2,1)S(1)}, u32[]{:S(2)}, u32[]{:S(2)}) async-start(bf16[128,16,128]{2,1,0:T(8,128)(2,1)} %bitcast.82), calls=%async_computation.1 | async-start | bytes 1048576 | tf_op jit(solution)/shard_map/all_to_all | solution.py:149
  122.0 1.4 copy-start.3
  124.2 36.0 %all-to-all-start.2 = ((bf16[128,16,128]{2,1,0:T(8,128)(2,1)}), bf16[128,16,128]{2,1,0:T(8,128)(2,1)}, u32[]{:S(2)}, u32[]{:S(2)}) async-start(bf16[128,16,128]{2,1,0:T(8,128)(2,1)} %slice.133), calls=%async_computation.2 | async-start | bytes 1048576 | tf_op jit(solution)/shard_map/all_to_all | solution.py:186
  133.3 1.1 copy-start.4
  134.5 1.0 copy-start.7
  135.5 1.0 copy-start.8
  158.2 1.2 copy-start.1
  159.4 0.8 copy-start.5
  161.4 0.8 copy-start.9
  177.5 3.0 collective-permute-start.5
  186.0 15.6 %collective-permute-start.6 = (f32[4,8,4096]{2,1,0:T(8,128)S(1)}, f32[4,8,4096]{2,1,0:T(8,128)S(1)}, u32[]{:S(2)}, u32[]{:S(2)}) collective-permute-start(f32[4,8,4096]{2,1,0:T(8,128)S(1)} %bitcast.96), channel_id=1, source_target_pairs={{0,4},{2,6},{4,0},{6,2},{8,12},{10,14},{12,8},{14,10},{16,20},{18,... | collective-permute-start | bytes 1572872 | tf_op jit(solution)/shard_map/ppermute | solution.py:201
  203.0 11.3 %all-to-all-start.4 = ((f32[4,8,4096]{2,1,0:T(8,128)}), f32[4,8,4096]{2,1,0:T(8,128)}, u32[]{:S(2)}, u32[]{:S(2)}) async-start(f32[4,8,4096]{2,1,0:T(8,128)} %fusion.10), calls=%async_computation.4 | async-start | bytes 1048576 | tf_op jit(solution)/shard_map/all_to_all | solution.py:207
  214.3 78.0 %all-to-all-start.3 = ((bf16[128,48,128]{2,1,0:T(8,128)(2,1)}), bf16[128,48,128]{2,1,0:T(8,128)(2,1)}, u32[]{:S(2)}, u32[]{:S(2)}) async-start(bf16[128,48,128]{2,1,0:T(8,128)(2,1)} %slice.134), calls=%async_computation.3 | async-start | bytes 3145728 | tf_op jit(solution)/shard_map/all_to_all | solution.py:187
  228.7 1.4 copy-start.2
  230.1 1.6 copy-start.10
  232.7 54.7 %collective-permute-start.2 = (bf16[1024,512]{1,0:T(8,128)(2,1)}, bf16[1024,512]{1,0:T(8,128)(2,1)}, u32[]{:S(2)}, u32[]{:S(2)}) collective-permute-start(bf16[1024,512]{1,0:T(8,128)(2,1)} %pad_maximum_fusion.3), channel_id=1, source_target_pairs={{0,1},{1,0},{2,3},{3,2},{4,5},{5,4},{6,7},{7,6},{8,9},{9,8},{10,11... | collective-permute-start | bytes 3145736 | tf_op jit(solution)/shard_map/ppermute | solution.py:110
  233.8 33.8 %collective-permute-start.4 = (bf16[2,512,256]{2,1,0:T(8,128)(2,1)}, bf16[2,512,256]{2,1,0:T(8,128)(2,1)}, u32[]{:S(2)}, u32[]{:S(2)}) collective-permute-start(bf16[2,512,256]{2,1,0:T(8,128)(2,1)} %pad_maximum_fusion.10), channel_id=1, source_target_pairs={{2,0},{4,2},{6,4},{8,6},{10,8},{12,10},{14,12},{16,14},{18,16},{20... | collective-permute-start | bytes 1572872 | tf_op jit(solution)/shard_map/ppermute | solution.py:175
  241.7 45.7 %collective-permute-start.3 = (bf16[512,512]{1,0:T(8,128)(2,1)}, bf16[512,512]{1,0:T(8,128)(2,1)}, u32[]{:S(2)}, u32[]{:S(2)}) collective-permute-start(bf16[512,512]{1,0:T(8,128)(2,1)} %constant_dynamic-slice_fusion), channel_id=1, source_target_pairs={{0,1},{1,0},{2,3},{3,2},{4,5},{5,4},{6,7},{7,6},{8,9},{9,8},{10,11... | collective-permute-start | bytes 1572872 | tf_op jit(solution)/shard_map/ppermute | solution.py:110
  242.3 28.3 %copy-start.11 = (bf16[2,64,8,2,128]{4,2,3,1,0:T(8,128)(2,1)S(1)}, bf16[2,64,8,2,128]{4,2,3,1,0:T(8,128)(2,1)}, u32[]{:S(2)}) copy-start(bf16[2,64,8,2,128]{4,2,3,1,0:T(8,128)(2,1)} %copy-done.9) | copy-start | bytes 1572868
  292.3 15.4 %all-to-all-start.5 = ((f32[8,1,4096]{2,1,0:T(1,128)}), f32[8,1,4096]{2,1,0:T(1,128)S(1)}, u32[]{:S(2)}, u32[]{:S(2)}) async-start(f32[8,1,4096]{2,1,0:T(1,128)} %all_to_all.26), calls=%async_computation.5 | async-start | bytes 262144 | tf_op jit(solution)/shard_map/all_to_all | solution.py:208
  299.3 1.0 copy-start.6
  299.4 2.0 copy-start.16
  299.4 2.0 copy-start.18
  300.3 2.1 copy-start.17

commit v2 on v1

v2 whole, which is shorter than its diff:
```python
import math

import jax
import jax.numpy as jnp
from jax import lax
from jax.experimental import pallas as pl
from jax.experimental.pallas import tpu as pltpu
from jax.sharding import PartitionSpec as P

HEAD_DIM = 64
STRIDE = 512
BLOCK = 64
TILE = 256
MASKED = -1e30
F32 = jnp.float32
BF16 = jnp.bfloat16
MESH = pl.DeviceIdType.MESH
Y, Z, XH, CORES = 4, 8, 2, 2
SEQ = Y * Z * XH * CORES


def dot(a, b):
    return jnp.dot(a, b, preferred_element_type=F32)


def pair_tile(q, k, v, d, allowed):
    nq = q.shape[0]
    qs = (q.astype(F32) * HEAD_DIM**-0.5).astype(BF16)
    q_t, d_t, k_t, v_t = (m.astype(F32).T.astype(BF16) for m in (qs, d, k, v))
    low = lax.broadcasted_iota(jnp.int32, (nq, 2 * HEAD_DIM), 1) < HEAD_DIM
    blank = jnp.zeros((HEAD_DIM, nq), BF16)
    nothing = jnp.zeros_like(q)
    outs, dqs, dk, dv = [], [], None, None
    for h in range(2):
        mine = slice(h * HEAD_DIM, (h + 1) * HEAD_DIM)

        def alone(m_t):
            return jnp.concatenate([m_t[mine], blank] if h == 0 else [blank, m_t[mine]], axis=0)

        scores = jnp.where(allowed, dot(k, alone(q_t)), MASKED)
        highest = jnp.max(scores, axis=0, keepdims=True)
        weights = jnp.exp(scores - highest)
        weights = weights * (1.0 / jnp.sum(weights, axis=0, keepdims=True))
        low_weights = weights.astype(BF16)
        out_t = dot(v_t[mine], low_weights).astype(BF16).astype(F32)
        delta = jnp.sum(out_t * d_t[mine].astype(F32), axis=0, keepdims=True)
        d_scores = (weights * (dot(v, alone(d_t)) - delta)).astype(BF16)
        outs.append(out_t)
        dqs.append(dot(k_t[mine], d_scores) * HEAD_DIM**-0.5)
        keep = low if h == 0 else jnp.logical_not(low)
        dk_h = dot(d_scores, jnp.where(keep, qs, nothing))
        dv_h = dot(low_weights, jnp.where(keep, d, nothing))
        dk = dk_h if dk is None else dk + dk_h
        dv = dv_h if dv is None else dv + dv_h
    return jnp.concatenate(outs, axis=0).T, jnp.concatenate(dqs, axis=0).T, dk, dv


def dot_nt(a, b):
    return lax.dot_general(a, b, (((1,), (1,)), ((), ())), preferred_element_type=F32)


def row_of(count, part, values):
    run = lax.broadcasted_iota(jnp.int32, (1, count), 1) // part
    row = jnp.zeros((1, count), jnp.int32)
    for i, value in enumerate(values):
        row = jnp.where(run == i, value, row)
    return row


def to_messages(x):
    grid = x.astype(F32).reshape(2, STRIDE // 8, 8, 128)
    return jnp.concatenate([grid[0], grid[1]], axis=1).astype(BF16)


def from_messages(m):
    grid = m.astype(F32)
    halves = [grid[:, 8 * r : 8 * r + 8].reshape(STRIDE, 128) for r in range(2)]
    return jnp.concatenate(halves, axis=0).astype(BF16)


def layer_kernel(
    q_ref, k_ref, v_ref, w_ref, g_ref, band_ref, reach_ref,
    out_ref, dq_ref, dk_ref, dv_ref, proj_ref,
    qkv_send, qkv_recv, col_d_send, col_d_recv, reach_all,
    g_other, w_other, rim, rim_send, rim_recv,
    d_att, g_t, dk_sum, dv_sum, wide, back,
    res_out, res_grad, got_out, got_grad, att, att_other,
    term, core_in, core_sum, x_in, x_sum, y_in, y_sum, z_in,
    send, recv,
):
    tokens, width = q_ref.shape
    half = width // 2
    me, head = lax.axis_index("seq"), lax.axis_index("head")
    core, x_hi, z, y = lax.rem(me, 2), lax.rem(me // 2, 2), lax.rem(me // 4, Z), me // (4 * Z)
    seq_at = lambda y, z, x_hi, core: ((y * Z + z) * XH + x_hi) * CORES + core

    def remote(src, dst, n, seq, other=None):
        return pltpu.make_async_remote_copy(
            src_ref=src, dst_ref=dst, send_sem=send.at[n], recv_sem=recv.at[n],
            device_id=(seq, head if other is None else other), device_id_type=MESH,
        )

    barrier = pltpu.get_barrier_semaphore()

    @pl.loop(1, SEQ)
    def _(i):
        pl.semaphore_signal(barrier, inc=1, device_id=(lax.rem(me + i, SEQ), head), device_id_type=MESH)

    pl.semaphore_signal(barrier, inc=1, device_id=(me, 1 - head), device_id_type=MESH)

    lane = lax.broadcasted_iota(jnp.int32, (1, 128), 1)
    mine_reach = row_of(128, 1, [reach_ref[i] for i in range(16)])
    mine_reach = mine_reach.astype(F32)
    reach_all[me] = mine_reach
    for t, ref in enumerate((q_ref, k_ref, v_ref)):
        for hp in range(2):
            lanes = slice(half + hp * 128, half + hp * 128 + 128)
            qkv_send[hp * 64 : hp * 64 + 64, 16 * t : 16 * t + 16, :] = to_messages(ref[:, lanes])
    pl.semaphore_wait(barrier, SEQ)

    swap_g = remote(g_ref, g_other, 0, me, 1 - head)
    swap_g.start()
    their_w = w_ref.at[:, pl.ds(pl.multiple_of((1 - head) * width, 128), width)]
    swap_w = remote(their_w, w_other, 1, me, 1 - head)

    @pl.loop(1, SEQ)
    def _(i):
        to = lax.rem(me + i, SEQ)
        remote(qkv_send.at[to], qkv_recv.at[me], 2, to).start()
        remote(reach_all.at[me], reach_all.at[me], 3, to).start()

    qkv_recv[me] = qkv_send[me]

    for t, ref in enumerate((k_ref, v_ref)):
        rim[t, STRIDE:, :] = ref[:, :half]
    rim_to = remote(rim.at[:, pl.ds(tokens, STRIDE)], rim.at[:, pl.ds(0, STRIDE)], 4, jnp.minimum(me + 1, SEQ - 1))

    @pl.when(me < SEQ - 1)
    def _():
        rim_to.start()

    @pl.when(me == 0)
    def _():
        rim[:, :STRIDE, :] = jnp.zeros((2, STRIDE, half), BF16)

    mine_c = pl.ds(pl.multiple_of(head * width, 128), width)
    other_c = pl.ds(pl.multiple_of((1 - head) * width, 128), width)

    def turn(ref, rows):
        for i in range(tokens // TILE):
            part = slice(i * TILE, i * TILE + TILE)
            g_t[rows, part] = ref[part, :].astype(F32).T.astype(BF16)

    turn(g_ref, mine_c)
    swap_g.wait()

    @pl.loop(0, tokens // TILE)
    def _(i):
        part = pl.ds(pl.multiple_of(i * TILE, TILE), TILE)
        d = dot_nt(g_ref[part, :], w_ref[:, mine_c]) + dot_nt(g_other[part, :], w_ref[:, other_c])
        d_att[part, :] = d.astype(BF16)

    for hp in range(2):
        lanes = slice(half + hp * 128, half + hp * 128 + 128)
        col_d_send[hp * 64 : hp * 64 + 64] = to_messages(d_att[:, lanes])

    @pl.loop(1, SEQ)
    def _(i):
        to = lax.rem(me + i, SEQ)
        remote(col_d_send.at[to], col_d_recv.at[me], 5, to).start()

    col_d_recv[me] = col_d_send[me]
    swap_w.start()
    turn(g_other, other_c)

    @pl.when(me < SEQ - 1)
    def _():
        rim_to.wait_send()

    @pl.when(me > 0)
    def _():
        rim_to.wait_recv()

    blocks = tokens // BLOCK
    span = TILE + STRIDE
    edge = jnp.where(me == 0, STRIDE, 0)
    for pair in range(2):
        lanes = slice(pair * 128, pair * 128 + 128)
        dk_sum[pair] = jnp.zeros((tokens + STRIDE, 128), F32)
        dv_sum[pair] = jnp.zeros((tokens + STRIDE, 128), F32)

    @pl.loop(0, tokens // TILE)
    def _(step):
        begin = pl.multiple_of(step * TILE, TILE)
        mine, span_at = pl.ds(begin, TILE), pl.ds(begin, span)
        key_at = lax.broadcasted_iota(jnp.int32, (span, TILE), 0)
        query_at = STRIDE + lax.broadcasted_iota(jnp.int32, (span, TILE), 1)
        block_at = query_at[:1] // BLOCK
        count = row_of(TILE, BLOCK, [band_ref[step * (TILE // BLOCK) + i] for i in range(TILE // BLOCK)])
        lowest = jnp.maximum((block_at - count + 1) * BLOCK, edge - begin)
        allowed = (key_at <= query_at) & (key_at >= lowest)
        for pair in range(2):
            lanes = slice(pair * 128, pair * 128 + 128)
            out, dq, dk, dv = pair_tile(
                q_ref[mine, lanes], rim[0, span_at, lanes], rim[1, span_at, lanes], d_att[mine, lanes], allowed
            )
            att[mine, lanes] = out.astype(BF16)
            dq_ref[mine, lanes] = dq.astype(BF16)
            dk_sum[pair, span_at, :] += dk
            dv_sum[pair, span_at, :] += dv

    for pair in range(2):
        lanes = slice(pair * 128, pair * 128 + 128)
        rim_send[0, :, lanes] = dk_sum[pair, :STRIDE, :].astype(BF16)
        rim_send[1, :, lanes] = dv_sum[pair, :STRIDE, :].astype(BF16)
    rim_back = remote(rim_send, rim_recv, 6, jnp.maximum(me - 1, 0))

    @pl.when(me > 0)
    def _():
        rim_back.start()

    @pl.when(me == SEQ - 1)
    def _():
        rim_recv[...] = jnp.zeros((2, STRIDE, half), BF16)

    def wait_all(src, dst, n):
        everyone = remote(src.at[pl.ds(0, SEQ - 1)], dst.at[pl.ds(0, SEQ - 1)], n, lax.rem(me + 1, SEQ))
        everyone.wait_send()
        everyone.wait_recv()

    wait_all(reach_all, reach_all, 3)
    wait_all(qkv_send, qkv_recv, 2)
    wait_all(col_d_send, col_d_recv, 5)
    for t in range(3):
        wide[t] = qkv_recv[:, 16 * t : 16 * t + 16, :].astype(F32).reshape(16 * SEQ, 128)
    wide[3] = col_d_recv[...].astype(F32).reshape(16 * SEQ, 128)
    table = reach_all[...].reshape(SEQ, 128).T
    block = lax.rem(me, 64) // 8
    row_at = lax.broadcasted_iota(jnp.int32, (128, SEQ), 0)
    reach = jnp.concatenate(
        [jnp.sum(jnp.where(row_at == block + 8 * r, table, 0.0), axis=0, keepdims=True) for r in range(2)], axis=1
    ).astype(jnp.int32)
    rows = 2 * SEQ

    def image_row(axis):
        i = lax.broadcasted_iota(jnp.int32, (rows, rows), axis)
        return 2 * lax.rem(i, SEQ) + i // SEQ

    @pl.loop(0, 8)
    def _(column):
        apart = image_row(1) - image_row(0)
        allowed = (apart >= 0) & (apart < reach)
        at = [pl.ds(column + 8 * r, SEQ, stride=16) for r in range(2)]
        q, k, v, d = (
            jnp.concatenate([wide[t, at[0], :], wide[t, at[1], :]], axis=0).astype(BF16) for t in range(4)
        )
        for t, value in enumerate(pair_tile(q, k, v, d, allowed)):
            for r in range(2):
                back[t, at[r], :] = value[r * SEQ : r * SEQ + SEQ]

    res_out[...] = back[0].reshape(SEQ, 16, 128).astype(BF16)

    @pl.loop(1, SEQ)
    def _(i):
        to = lax.rem(me + i, SEQ)
        remote(res_out.at[to], got_out.at[me], 7, to).start()

    got_out[me] = res_out[me]
    for t in range(3):
        res_grad[:, 16 * t : 16 * t + 16, :] = back[t + 1].reshape(SEQ, 16, 128).astype(BF16)

    @pl.loop(1, SEQ)
    def _(i):
        to = lax.rem(me + i, SEQ)
        remote(res_grad.at[to], got_grad.at[me], 8, to).start()

    got_grad[me] = res_grad[me]

    wait_all(res_out, got_out, 7)
    for hp in range(2):
        att[:, half + hp * 128 : half + hp * 128 + 128] = from_messages(got_out[hp * 64 : hp * 64 + 64])
    swap_att = remote(att, att_other, 9, me, 1 - head)
    swap_att.start()

    @pl.loop(0, 2 * width // TILE)
    def _(i):
        part = pl.ds(pl.multiple_of(i * TILE, TILE), TILE)
        term[pl.ds(8 * i, 8)] = dot(g_t[part, :], att[...]).reshape(8, XH, CORES, 8, width)

    copy = remote(term.at[:, :, 1 - core], core_in, 10, me + 1 - 2 * core)
    copy.start()
    copy.wait()

    @pl.loop(0, Y * Z)
    def _(i):
        core_sum[i] = term[i, :, core] + core_in[i]

    copy = remote(core_sum.at[:, 1 - x_hi], x_in, 11, me + 2 - 4 * x_hi)
    copy.start()
    swap_w.wait()
    swap_att.wait()

    @pl.loop(0, tokens // TILE)
    def _(i):
        part = pl.ds(pl.multiple_of(i * TILE, TILE), TILE)
        total = dot(att[part, :], w_ref[:, mine_c]) + dot(att_other[part, :], w_other[...])
        out_ref[part, :] = total.astype(BF16)

    copy.wait()

    @pl.loop(0, Y * Z)
    def _(i):
        x_sum[i] = core_sum[i, x_hi] + x_in[i]

    for i in range(1, Y):
        to = lax.rem(y + i, Y)
        remote(x_sum.at[pl.ds(to * Z, Z)], y_in.at[y], 12, seq_at(to, z, x_hi, core)).start()
    y_in[y] = x_sum[pl.ds(y * Z, Z)]
    everyone = remote(y_in.at[pl.ds(0, Y - 1)], y_in.at[pl.ds(0, Y - 1)], 12, seq_at(lax.rem(y + 1, Y), z, x_hi, core))
    everyone.wait_send()
    everyone.wait_recv()
    y_sum[...] = y_in[0] + y_in[1] + y_in[2] + y_in[3]
    for i in range(1, Z):
        to = lax.rem(z + i, Z)
        remote(y_sum.at[to], z_in.at[z], 13, seq_at(y, to, x_hi, core)).start()
    z_in[z] = y_sum[z]
    everyone = remote(z_in.at[pl.ds(0, Z - 1)], z_in.at[pl.ds(0, Z - 1)], 13, seq_at(y, lax.rem(z + 1, Z), x_hi, core))
    everyone.wait_send()
    everyone.wait_recv()
    total = z_in[0]
    for i in range(1, Z):
        total = total + z_in[i]
    proj_ref[...] = (total * (1.0 / math.sqrt(tokens * SEQ))).T

    @pl.when(me > 0)
    def _():
        rim_back.wait_send()

    @pl.when(me < SEQ - 1)
    def _():
        rim_back.wait_recv()

    for t, (ref, sums) in enumerate(((dk_ref, dk_sum), (dv_ref, dv_sum))):
        for pair in range(2):
            lanes = slice(pair * 128, pair * 128 + 128)
            ref[:STRIDE, lanes] = sums[pair, STRIDE:tokens, :].astype(BF16)
            ref[STRIDE:, lanes] = (sums[pair, tokens:, :] + rim_recv[t, :, lanes].astype(F32)).astype(BF16)
    wait_all(res_grad, got_grad, 8)
    for t, ref in enumerate((dq_ref, dk_ref, dv_ref)):
        for hp in range(2):
            lanes = slice(half + hp * 128, half + hp * 128 + 128)
            ref[:, lanes] = from_messages(got_grad[hp * 64 : hp * 64 + 64, 16 * t : 16 * t + 16, :])


def local(queries, key_rows, value_rows, out_proj, grad_out, band_blocks, column_reach):
    tokens, width = queries.shape
    half = width // 2
    low = lambda *shape: pltpu.VMEM(shape, BF16)
    full = lambda *shape: pltpu.VMEM(shape, F32)
    vmem, smem = pl.BlockSpec(memory_space=pltpu.VMEM), pl.BlockSpec(memory_space=pltpu.SMEM)
    result = jax.ShapeDtypeStruct((tokens, width), BF16)
    return pl.pallas_call(
        layer_kernel,
        out_shape=(result, result, result, result, jax.ShapeDtypeStruct((width, 2 * width // SEQ), F32)),
        in_specs=[vmem] * 5 + [smem] * 2,
        out_specs=(vmem,) * 5,
        scratch_shapes=[
            low(SEQ, 48, 128), low(SEQ, 48, 128), low(SEQ, 16, 128), low(SEQ, 16, 128), full(SEQ, 1, 128),
            low(tokens, width), low(width, width), low(2, tokens + STRIDE, half), low(2, STRIDE, half),
            low(2, STRIDE, half),
            low(tokens, width), low(2 * width, tokens), full(2, tokens + STRIDE, 128), full(2, tokens + STRIDE, 128),
            full(4, 16 * SEQ, 128), full(4, 16 * SEQ, 128),
            low(SEQ, 16, 128), low(SEQ, 48, 128), low(SEQ, 16, 128), low(SEQ, 48, 128), low(tokens, width),
            low(tokens, width),
            full(Y * Z, XH, CORES, 8, width), full(Y * Z, XH, 8, width), full(Y * Z, XH, 8, width),
            full(Y * Z, 8, width), full(Y * Z, 8, width), full(Y, Z, 8, width), full(Z, 8, width), full(Z, 8, width),
            pltpu.SemaphoreType.DMA((14,)), pltpu.SemaphoreType.DMA((14,)),
        ],
        compiler_params=pltpu.CompilerParams(
            collective_id=0, has_side_effects=True, vmem_limit_bytes=60 * 2**20
        ),
        cost_estimate=pl.CostEstimate(flops=2 * 10**10, bytes_accessed=10 * 2**20, transcendentals=0),
    )(queries, key_rows, value_rows, out_proj, grad_out, band_blocks, column_reach)


def solution(mesh):
    tokens = P("seq", "head")
    return jax.shard_map(
        local,
        mesh=mesh,
        in_specs=(tokens, tokens, tokens, P("head", None), tokens, P("seq"), P("seq")),
        out_specs=(tokens, tokens, tokens, tokens, P("head", "seq")),
        check_vma=False,
    )
```

time: 310 us -> 192 us (0.62)
  Pallas kernels: 35.1 us -> 182 us
  waiting for transfers between devices: 118 us -> 0 us
  starting transfers between devices: 82.7 us -> 0 us
  other arithmetic: 28.3 us -> 0 us
  local copies, waits for them, and re-layouts: 33.9 us -> 8.19 us
  matrix products: 9.17 us -> 0 us
    pallas_call x2 -> x1, Pallas kernels: 35.1 us -> 182 us  [local(): pl.pallas_call(layer_kernel, out_shape=(result, result, result, result, j...]
    ppermute x7 -> x0, waiting for transfers between devices: 95.7 us -> none  [the longest x3 55 us: swap_head(): return lax.ppermute(x, 'head', [(0, 1), (1, 0)])]
    all_to_all x6 -> x0, starting transfers between devices: 69 us -> none  [the longest x1 19.3 us: local(): lax.all_to_all(to_messages(d_attended, half), 'seq', 0, 0, tiled=True)]
    all_to_all x6 -> x0, waiting for transfers between devices: 22.6 us -> none  [the longest x1 14.7 us: local(): lax.all_to_all(to_messages(d_attended, half), 'seq', 0, 0, tiled=True)]
    ppermute x7 -> x0, starting transfers between devices: 13.7 us -> none  [the longest x1 7.04 us: local(): lax.ppermute(rim_back, 'seq', [(i + 1, i) for i in range(seq_devices - 1)])]
    slice x9 -> x0, local copies, waits for them, and re-layouts: 9.83 us -> none  [the longest x1 2.66 us: local(): grads_back = lax.all_to_all(column_results[:, 16:], 'seq', 0, 0, tiled=True)]
    dot_general x4 -> x0, matrix products: 9.17 us -> none  [the longest x1 4.15 us: local(): lax.dot_general(grad_all, attended, (((0,), (0,)), ((), ())), preferred_e...]
    slice x2 -> x0, other arithmetic: 6.72 us -> none  [halve(): keep = jnp.where(bit == 0, parts[:, :, 0], parts[:, :, 1])]
  transfers between devices with their start and end apart: 13 -> 0, of which waited for: 8 -> 0; matrix products, arithmetic and copies ran while one was open for 10% -> 0% of each run, Pallas kernels for 7% -> 0%
where the time goes in v2:
time: 192 us; the launch traced here: 191 us
  Pallas kernels  182 us (95%)
  local copies, waits for them, and re-layouts  8.19 us (4%)
    pallas_call x1, Pallas kernels, local(): pl.pallas_call(layer_kernel, out_shape=(result, result, result, result, j...  182 us
    unnamed x10, local copies, waits for them, and re-layouts  6.53 us

profile of v2, /device:TPU:16, one launch (start us, length us, event | category | flops | bytes accessed | tf_op | source)
XLA Modules:
  0.0 191.1 jit_solution(3719907582224937537)
XLA Ops:
  0.6 182.3 %shard_map.110 = (bf16[1024,512]{1,0:T(8,128)(2,1)}, bf16[1024,512]{1,0:T(8,128)(2,1)}, bf16[1024,512]{1,0:T(8,128)(2,1)}, bf16[1024,512]{1,0:T(8,128)(2,1)}, f32[512,8]{1,0:T(8,128)}) custom-call(bf16[1024,512]{1,0:T(8,128)(2,1)} %q_ref.1, bf16[1024,512]{1,0:T(8,128)(2,1)} %k_ref.1, bf16[1024,512]{1,0:T(8,128)(2,1)} %v_ref.1, bf16[512,1024]{1,0:T(8,128)(2,1)} %w_ref.1, ...), custom_call_target="tpu_custom_call" | custom-call | flops 20000000000 | bytes 10485760 | tf_op jit(solution)/shard_map/pallas_call | solution.py:362
  182.9 1.7 copy.12
  184.6 0.0 copy-start.2
  184.6 2.4 %copy.17 = bf16[1024,512]{1,0:T(8,128)(2,1)} copy(bf16[1024,512]{1,0:T(8,128)(2,1)} %get-tuple-element.15) | data formatting | bytes 2097152
  186.9 0.0 copy-done.2
  186.9 0.0 copy-start.1
  186.9 1.0 copy.18
  187.9 0.6 copy-done.1
  188.5 0.0 copy-start
  188.6 1.0 copy.19
  189.5 0.6 copy-done
  190.2 1.0 copy.20
Async XLA Ops:
  184.6 2.4 %copy-start.2 = (bf16[1024,512]{1,0:T(8,128)(2,1)S(1)}, bf16[1024,512]{1,0:T(8,128)(2,1)}, u32[]{:S(2)}) copy-start(bf16[1024,512]{1,0:T(8,128)(2,1)} %get-tuple-element.16) | copy-start | bytes 3145732
  186.9 1.6 copy-start.1
  188.5 1.6 copy-start

commit v3 on v2

v3 whole, which is shorter than its diff:
```python
import math

import jax
import jax.numpy as jnp
from jax import lax
from jax.experimental import pallas as pl
from jax.experimental.pallas import tpu as pltpu
from jax.sharding import PartitionSpec as P

HEAD_DIM = 64
STRIDE = 512
BLOCK = 64
TILE = 256
MASKED = -1e30
F32 = jnp.float32
BF16 = jnp.bfloat16
MESH = pl.DeviceIdType.MESH
Y, Z, XH, CORES = 4, 8, 2, 2
SEQ = Y * Z * XH * CORES


def dot(a, b):
    return jnp.dot(a, b, preferred_element_type=F32)


def turned(m):
    return m.astype(F32).T.astype(BF16)


def scaled(q):
    return (q.astype(F32) * HEAD_DIM**-0.5).astype(BF16)


def head_rows(h):
    return slice(h * HEAD_DIM, (h + 1) * HEAD_DIM)


def alone(m_t, h):
    blank = jnp.zeros((HEAD_DIM, m_t.shape[1]), BF16)
    return jnp.concatenate([m_t[head_rows(h)], blank] if h == 0 else [blank, m_t[head_rows(h)]], axis=0)


def pair_scores(q_t, k, allowed, h):
    return jnp.where(allowed, dot(k, alone(q_t, h)), MASKED)


def pair_forward(q, k, v, allowed):
    q_t, v_t = turned(scaled(q)), turned(v)
    outs, all_weights, stats = [], [], []
    for h in range(2):
        scores = pair_scores(q_t, k, allowed, h)
        highest = jnp.max(scores, axis=0, keepdims=True)
        weights = jnp.exp(scores - highest)
        share = 1.0 / jnp.sum(weights, axis=0, keepdims=True)
        weights = weights * share
        outs.append(dot(v_t[head_rows(h)], weights.astype(BF16)).astype(BF16).astype(F32))
        all_weights.append(weights)
        stats.append((highest, share))
    return jnp.concatenate(outs, axis=0), all_weights, stats


def pair_backward(q, k, v, d, out_t, weights_of):
    qs = scaled(q)
    q_t, d_t, k_t = turned(qs), turned(d), turned(k)
    first = lax.broadcasted_iota(jnp.int32, q.shape, 1) < HEAD_DIM
    nothing = jnp.zeros_like(q)
    dqs, dk, dv = [], None, None
    for h in range(2):
        mine = head_rows(h)
        weights = weights_of(h, q_t)
        delta = jnp.sum(out_t[mine] * d_t[mine].astype(F32), axis=0, keepdims=True)
        d_scores = (weights * (dot(v, alone(d_t, h)) - delta)).astype(BF16)
        dqs.append(dot(k_t[mine], d_scores) * HEAD_DIM**-0.5)
        keep = first if h == 0 else jnp.logical_not(first)
        dk_h = dot(d_scores, jnp.where(keep, qs, nothing))
        dv_h = dot(weights.astype(BF16), jnp.where(keep, d, nothing))
        dk = dk_h if dk is None else dk + dk_h
        dv = dv_h if dv is None else dv + dv_h
    return jnp.concatenate(dqs, axis=0).T, dk, dv


def dot_nt(a, b):
    return lax.dot_general(a, b, (((1,), (1,)), ((), ())), preferred_element_type=F32)


def row_of(count, part, values):
    run = lax.broadcasted_iota(jnp.int32, (1, count), 1) // part
    row = jnp.zeros((1, count), jnp.int32)
    for i, value in enumerate(values):
        row = jnp.where(run == i, value, row)
    return row


def to_messages(x):
    grid = x.astype(F32).reshape(2, STRIDE // 8, 8, 128)
    return jnp.concatenate([grid[0], grid[1]], axis=1).astype(BF16)


def from_messages(m):
    grid = m.astype(F32)
    halves = [grid[:, 8 * r : 8 * r + 8].reshape(STRIDE, 128) for r in range(2)]
    return jnp.concatenate(halves, axis=0).astype(BF16)


def layer_kernel(
    q_in, k_in, v_in, w_in, g_in, band_ref, reach_ref,
    out_to, dq_to, dk_to, dv_to, got_grad, proj_ref,
    q_ref, k_ref, v_ref, w_ref, g_ref, out_ref, dq_ref, dk_ref, dv_ref,
    qkv_send, qkv_recv, col_d_send, col_d_recv, reach_all,
    g_other, w_other, rim, rim_send, rim_recv,
    d_att, g_t, dk_sum, dv_sum, stats, wide, back, col_weights, col_out_t,
    res_out, res_grad, got_out, att, att_other,
    term, core_in, core_sum, y_in, y_sum, x_in, x_sum, z_in,
    send, recv, near,
):
    tokens, width = q_ref.shape
    half = width // 2
    me, head = lax.axis_index("seq"), lax.axis_index("head")
    core, x_hi, z, y = lax.rem(me, 2), lax.rem(me // 2, 2), lax.rem(me // 4, Z), me // (4 * Z)

    def seq_at(y, z, x_hi, core):
        return ((y * Z + z) * XH + x_hi) * CORES + core

    def remote(src, dst, n, seq, other=None):
        return pltpu.make_async_remote_copy(
            src_ref=src, dst_ref=dst, send_sem=send.at[n], recv_sem=recv.at[n],
            device_id=(seq, head if other is None else other), device_id_type=MESH,
        )

    def exchange(start):
        place = (me // 4) * 2 + core

        def peer(i, side):
            to = lax.rem(place + i, SEQ // 2)
            return (to // 2) * 4 + side * 2 + lax.rem(to, 2)

        @pl.loop(1, SEQ // 2)
        def _(i):
            start(peer(i, x_hi))

        @pl.loop(0, SEQ // 2)
        def _(i):
            start(peer(i, 1 - x_hi))

    def wait_all(src, dst, n):
        everyone = remote(src.at[pl.ds(0, SEQ - 1)], dst.at[pl.ds(0, SEQ - 1)], n, lax.rem(me + 1, SEQ))
        everyone.wait_send()
        everyone.wait_recv()

    loads = [
        pltpu.make_async_copy(a, b, near.at[i])
        for i, (a, b) in enumerate(((k_in, k_ref), (v_in, v_ref), (q_in, q_ref), (g_in, g_ref), (w_in, w_ref)))
    ]
    for load in loads:
        load.start()

    def store(n, src, dst):
        copy = pltpu.make_async_copy(src, dst, near.at[len(loads) + n])
        copy.start()
        return copy

    barrier = pltpu.get_barrier_semaphore()
    pl.semaphore_signal(barrier, inc=1, device_id=(me, 1 - head), device_id_type=MESH)

    @pl.loop(1, SEQ)
    def _(i):
        pl.semaphore_signal(barrier, inc=1, device_id=(lax.rem(me + i, SEQ), head), device_id_type=MESH)

    reach_all[me] = row_of(128, 1, [reach_ref[i] for i in range(16)]).astype(F32)
    for load in loads:
        load.wait()
    for t, ref in enumerate((q_ref, k_ref, v_ref)):
        for hp in range(2):
            lanes = slice(half + hp * 128, half + hp * 128 + 128)
            qkv_send[hp * 64 : hp * 64 + 64, 16 * t : 16 * t + 16, :] = to_messages(ref[:, lanes])
    for t, ref in enumerate((k_ref, v_ref)):
        rim[t, STRIDE:, :] = ref[:, :half]
    pl.semaphore_wait(barrier, SEQ)

    swap_g = remote(g_ref, g_other, 0, me, 1 - head)
    swap_g.start()

    rim_to = remote(rim.at[:, pl.ds(tokens, STRIDE)], rim.at[:, pl.ds(0, STRIDE)], 4, jnp.minimum(me + 1, SEQ - 1))

    @pl.when(me < SEQ - 1)
    def _():
        rim_to.start()

    @pl.when(me == 0)
    def _():
        rim[:, :STRIDE, :] = jnp.zeros((2, STRIDE, half), BF16)

    def start(to):
        remote(qkv_send.at[to], qkv_recv.at[me], 2, to).start()
        remote(reach_all.at[me], reach_all.at[me], 3, to).start()

    exchange(start)
    qkv_recv[me] = qkv_send[me]

    mine_c = pl.ds(pl.multiple_of(head * width, 128), width)
    other_c = pl.ds(pl.multiple_of((1 - head) * width, 128), width)

    def turn(ref, rows):
        for i in range(tokens // TILE):
            part = slice(i * TILE, i * TILE + TILE)
            g_t[rows, part] = turned(ref[part, :])

    turn(g_ref, mine_c)

    @pl.when(me < SEQ - 1)
    def _():
        rim_to.wait_send()

    @pl.when(me > 0)
    def _():
        rim_to.wait_recv()

    span = TILE + STRIDE
    edge = jnp.where(me == 0, STRIDE, 0)

    def band_step(step):
        begin = pl.multiple_of(step * TILE, TILE)
        key_at = lax.broadcasted_iota(jnp.int32, (span, TILE), 0)
        query_at = STRIDE + lax.broadcasted_iota(jnp.int32, (span, TILE), 1)
        count = row_of(TILE, BLOCK, [band_ref[step * (TILE // BLOCK) + i] for i in range(TILE // BLOCK)])
        lowest = jnp.maximum((query_at[:1] // BLOCK - count + 1) * BLOCK, edge - begin)
        return pl.ds(begin, TILE), pl.ds(begin, span), (key_at <= query_at) & (key_at >= lowest)

    pairs = [slice(pair * 128, pair * 128 + 128) for pair in range(2)]

    @pl.loop(0, tokens // TILE)
    def _(step):
        mine, span_at, allowed = band_step(step)
        for pair, lanes in enumerate(pairs):
            out_t, _, rows = pair_forward(q_ref[mine, lanes], rim[0, span_at, lanes], rim[1, span_at, lanes], allowed)
            att[mine, lanes] = out_t.T.astype(BF16)
            stats[step, 4 * pair : 4 * pair + 4, :] = jnp.concatenate([*rows[0], *rows[1]], axis=0)

    swap_g.wait()

    @pl.loop(0, tokens // TILE)
    def _(i):
        part = pl.ds(pl.multiple_of(i * TILE, TILE), TILE)
        d = dot_nt(g_ref[part, :], w_ref[:, mine_c]) + dot_nt(g_other[part, :], w_ref[:, other_c])
        d_att[part, :] = d.astype(BF16)

    for hp in range(2):
        lanes = slice(half + hp * 128, half + hp * 128 + 128)
        col_d_send[hp * 64 : hp * 64 + 64] = to_messages(d_att[:, lanes])
    exchange(lambda to: remote(col_d_send.at[to], col_d_recv.at[me], 5, to).start())
    col_d_recv[me] = col_d_send[me]

    part_w = pl.ds(pl.multiple_of(core * (width // 2), 16), width // 2)
    swap_w = remote(w_ref.at[part_w, other_c], w_other.at[part_w], 1, me, 1 - head)
    swap_w.start()
    share_w = remote(w_other.at[part_w], w_other.at[part_w], 6, me + 1 - 2 * core)
    swap_band = remote(att.at[:, pl.ds(0, half)], att_other.at[:, pl.ds(0, half)], 9, me, 1 - head)
    swap_band.start()
    turn(g_other, other_c)

    def sum_core(n):
        @pl.loop(0, Y)
        def _(i):
            part = pl.ds(pl.multiple_of(i * TILE, TILE), TILE)
            term[n, i] = dot(g_t[part, :], att[:, n * half : n * half + half]).reshape(Z, XH, CORES, 8, half)

        copy = remote(term.at[n, :, :, :, 1 - core], core_in.at[n], 10 + 4 * n, me + 1 - 2 * core)
        copy.start()
        return copy

    def sum_y(n, copy):
        copy.wait()

        @pl.loop(0, Y)
        def _(i):
            core_sum[n, i] = term[n, i, :, :, core] + core_in[n, i]

        for i in range(1, Y):
            to = lax.rem(y + i, Y)
            remote(core_sum.at[n, to], y_in.at[n, y], 11 + 4 * n, seq_at(to, z, x_hi, core)).start()
        y_in[n, y] = core_sum[n, y]
        some = y_in.at[n, pl.ds(0, Y - 1)]
        return remote(some, some, 11 + 4 * n, seq_at(lax.rem(y + 1, Y), z, x_hi, core))

    def sum_x(n, copy):
        copy.wait_send()
        copy.wait_recv()
        y_sum[n] = y_in[n, 0] + y_in[n, 1] + y_in[n, 2] + y_in[n, 3]
        copy = remote(y_sum.at[n, :, 1 - x_hi], x_in.at[n], 12 + 4 * n, me + 2 - 4 * x_hi)
        copy.start()
        return copy

    def sum_z(n, copy):
        copy.wait()
        x_sum[n] = y_sum[n, :, x_hi] + x_in[n]
        for i in range(1, Z):
            to = lax.rem(z + i, Z)
            remote(x_sum.at[n, to], z_in.at[n, z], 13 + 4 * n, seq_at(y, to, x_hi, core)).start()
        z_in[n, z] = x_sum[n, z]
        some = z_in.at[n, pl.ds(0, Z - 1)]
        return remote(some, some, 13 + 4 * n, seq_at(y, lax.rem(z + 1, Z), x_hi, core))

    def sum_end(n, copy):
        copy.wait_send()
        copy.wait_recv()
        total = z_in[n, 0]
        for i in range(1, Z):
            total = total + z_in[n, i]
        proj_ref[:, n * half : n * half + half] = total * (1.0 / math.sqrt(tokens * SEQ))

    band_sum = sum_core(0)

    wait_all(reach_all, reach_all, 3)
    wait_all(qkv_send, qkv_recv, 2)
    for t in range(3):
        wide[t] = qkv_recv[:, 16 * t : 16 * t + 16, :].astype(F32).reshape(16 * SEQ, 128)
    table = reach_all[...].reshape(SEQ, 128).T
    block = lax.rem(me, 64) // 8
    row_at = lax.broadcasted_iota(jnp.int32, (128, SEQ), 0)
    reach = jnp.concatenate(
        [jnp.sum(jnp.where(row_at == block + 8 * r, table, 0.0), axis=0, keepdims=True) for r in range(2)], axis=1
    ).astype(jnp.int32)
    rows = 2 * SEQ

    def image_row(axis):
        i = lax.broadcasted_iota(jnp.int32, (rows, rows), axis)
        return 2 * lax.rem(i, SEQ) + i // SEQ

    def column_rows(column):
        return [pl.ds(column + 8 * r, SEQ, stride=16) for r in range(2)]

    def column_of(ts, column):
        at = column_rows(column)
        return [jnp.concatenate([wide[t, at[0], :], wide[t, at[1], :]], axis=0).astype(BF16) for t in ts]

    @pl.loop(0, 8)
    def _(column):
        apart = image_row(1) - image_row(0)
        allowed = (apart >= 0) & (apart < reach)
        out_t, weights, _ = pair_forward(*column_of(range(3), column), allowed)
        col_out_t[column] = out_t
        for h in range(2):
            col_weights[column, h] = weights[h]
        out = out_t.T
        for r, at in enumerate(column_rows(column)):
            back[at, :] = out[r * SEQ : r * SEQ + SEQ]

    res_out[...] = back[...].reshape(SEQ, 16, 128).astype(BF16)
    exchange(lambda to: remote(res_out.at[to], got_out.at[me], 7, to).start())
    got_out[me] = res_out[me]
    band_sum = sum_y(0, band_sum)
    swap_w.wait()
    share_w.start()

    wait_all(col_d_send, col_d_recv, 5)
    wide[3] = col_d_recv[...].astype(F32).reshape(16 * SEQ, 128)

    @pl.loop(0, 8)
    def _(column):
        values = pair_backward(
            *column_of(range(4), column), col_out_t[column], lambda h, q_t: col_weights[column, h]
        )
        for t, value in enumerate(values):
            for r, at in enumerate(column_rows(column)):
                wide[t, at, :] = value[r * SEQ : r * SEQ + SEQ]

    for t in range(3):
        res_grad[:, 16 * t : 16 * t + 16, :] = wide[t].reshape(SEQ, 16, 128).astype(BF16)
    exchange(lambda to: remote(res_grad.at[to], got_grad.at[me], 8, to).start())
    stores = [store(0, res_grad.at[me], got_grad.at[me])]
    band_sum = sum_x(0, band_sum)

    wait_all(res_out, got_out, 7)
    for hp in range(2):
        att[:, half + hp * 128 : half + hp * 128 + 128] = from_messages(got_out[hp * 64 : hp * 64 + 64])
    swap_column = remote(att.at[:, pl.ds(half, half)], att_other.at[:, pl.ds(half, half)], 18, me, 1 - head)
    swap_column.start()
    column_sum = sum_core(1)

    for pair in range(2):
        dk_sum[pair] = jnp.zeros((tokens + STRIDE, 128), F32)
        dv_sum[pair] = jnp.zeros((tokens + STRIDE, 128), F32)

    def band_backward(step):
        mine, span_at, allowed = band_step(step)
        for pair, lanes in enumerate(pairs):
            k = rim[0, span_at, lanes]

            def weights_of(h, q_t):
                at = 4 * pair + 2 * h
                highest, share = stats[step, at : at + 1, :], stats[step, at + 1 : at + 2, :]
                return jnp.exp(pair_scores(q_t, k, allowed, h) - highest) * share

            dq, dk, dv = pair_backward(
                q_ref[mine, lanes], k, rim[1, span_at, lanes], d_att[mine, lanes],
                att[mine, lanes].astype(F32).T, weights_of,
            )
            dq_ref[mine, lanes] = dq.astype(BF16)
            dk_sum[pair, span_at, :] += dk
            dv_sum[pair, span_at, :] += dv

    pl.loop(0, 2)(band_backward)
    for pair, lanes in enumerate(pairs):
        rim_send[0, :, lanes] = dk_sum[pair, :STRIDE, :].astype(BF16)
        rim_send[1, :, lanes] = dv_sum[pair, :STRIDE, :].astype(BF16)
    rim_back = remote(rim_send, rim_recv, 19, jnp.maximum(me - 1, 0))

    @pl.when(me > 0)
    def _():
        rim_back.start()

    @pl.when(me == SEQ - 1)
    def _():
        rim_recv[...] = jnp.zeros((2, STRIDE, half), BF16)

    column_sum = sum_y(1, column_sum)
    band_sum = sum_z(0, band_sum)
    pl.loop(2, tokens // TILE)(band_backward)
    column_sum = sum_x(1, column_sum)
    sum_end(0, band_sum)
    share_w.wait()
    swap_band.wait()
    swap_column.wait()

    @pl.loop(0, tokens // TILE)
    def _(i):
        part = pl.ds(pl.multiple_of(i * TILE, TILE), TILE)
        total = dot(att[part, :], w_ref[:, mine_c]) + dot(att_other[part, :], w_other[...])
        out_ref[part, :] = total.astype(BF16)

    stores.append(store(1, out_ref, out_to))
    stores.append(store(2, dq_ref, dq_to))
    column_sum = sum_z(1, column_sum)

    @pl.when(me > 0)
    def _():
        rim_back.wait_send()

    @pl.when(me < SEQ - 1)
    def _():
        rim_back.wait_recv()

    for t, (ref, sums) in enumerate(((dk_ref, dk_sum), (dv_ref, dv_sum))):
        for pair, lanes in enumerate(pairs):
            ref[:STRIDE, lanes] = sums[pair, STRIDE:tokens, :].astype(BF16)
            ref[STRIDE:, lanes] = (sums[pair, tokens:, :] + rim_recv[t, :, lanes].astype(F32)).astype(BF16)
    stores.append(store(3, dk_ref, dk_to))
    stores.append(store(4, dv_ref, dv_to))
    sum_end(1, column_sum)
    for copy in stores:
        copy.wait()
    wait_all(res_grad, got_grad, 8)


def result_kernel(out_ref, dq_ref, dk_ref, dv_ref, got_ref, out, dq, dk, dv, got, whole, sem):
    half = dq_ref.shape[1]
    loads, stores = [], []
    for t, band in enumerate((dq_ref, dk_ref, dv_ref)):
        part = pl.ds(16 * t, 16)
        loads.append(pltpu.make_async_copy(got_ref.at[:, part], got.at[:, part], sem.at[2 * t]))
        loads.append(pltpu.make_async_copy(band, whole.at[t, :, pl.ds(0, half)], sem.at[2 * t + 1]))
    loads.append(pltpu.make_async_copy(out_ref, whole.at[3], sem.at[6]))
    for load in loads:
        load.start()
    for t, result in enumerate((dq, dk, dv)):
        loads[2 * t].wait()
        for hp in range(2):
            lanes = slice(half + hp * 128, half + hp * 128 + 128)
            whole[t, :, lanes] = from_messages(got[hp * 64 : hp * 64 + 64, 16 * t : 16 * t + 16, :])
        loads[2 * t + 1].wait()
        stores.append(pltpu.make_async_copy(whole.at[t], result, sem.at[7 + t]))
        stores[-1].start()
    loads[6].wait()
    stores.append(pltpu.make_async_copy(whole.at[3], out, sem.at[10]))
    stores[-1].start()
    for store in stores:
        store.wait()


def local(queries, key_rows, value_rows, out_proj, grad_out, band_blocks, column_reach):
    tokens, width = queries.shape
    half = width // 2
    low = lambda *shape: pltpu.VMEM(shape, BF16)
    full = lambda *shape: pltpu.VMEM(shape, F32)
    vmem, smem = pl.BlockSpec(memory_space=pltpu.VMEM), pl.BlockSpec(memory_space=pltpu.SMEM)
    any_place = pl.BlockSpec(memory_space=pl.ANY)
    shape = jax.ShapeDtypeStruct
    result, banded = shape((tokens, width), BF16), shape((tokens, half), BF16)
    *parts, proj_grad = pl.pallas_call(
        layer_kernel,
        out_shape=(result, banded, banded, banded, shape((SEQ, 48, 128), BF16), shape((2 * width // SEQ, width), F32)),
        in_specs=[any_place] * 5 + [smem] * 2,
        out_specs=(any_place,) * 5 + (vmem,),
        scratch_shapes=[
            low(tokens, width), low(tokens, width), low(tokens, width), low(width, 2 * width), low(tokens, width),
            low(tokens, width), low(tokens, half), low(tokens, half), low(tokens, half),
            low(SEQ, 48, 128), low(SEQ, 48, 128), low(SEQ, 16, 128), low(SEQ, 16, 128), full(SEQ, 1, 128),
            low(tokens, width), low(width, width), low(2, tokens + STRIDE, half), low(2, STRIDE, half),
            low(2, STRIDE, half),
            low(tokens, width), low(2 * width, tokens), full(2, tokens + STRIDE, 128), full(2, tokens + STRIDE, 128),
            full(tokens // TILE, 8, TILE), full(4, 16 * SEQ, 128), full(16 * SEQ, 128), full(8, 2, 2 * SEQ, 2 * SEQ),
            full(8, 128, 2 * SEQ),
            low(SEQ, 16, 128), low(SEQ, 48, 128), low(SEQ, 16, 128), low(tokens, width), low(tokens, width),
            full(2, Y, Z, XH, CORES, 8, half), full(2, Y, Z, XH, 8, half), full(2, Y, Z, XH, 8, half),
            full(2, Y, Z, XH, 8, half), full(2, Z, XH, 8, half), full(2, Z, 8, half), full(2, Z, 8, half),
            full(2, Z, 8, half),
            pltpu.SemaphoreType.DMA((20,)), pltpu.SemaphoreType.DMA((20,)), pltpu.SemaphoreType.DMA((10,)),
        ],
        compiler_params=pltpu.CompilerParams(
            collective_id=0, has_side_effects=True, vmem_limit_bytes=56 * 2**20
        ),
        cost_estimate=pl.CostEstimate(flops=2 * 10**10, bytes_accessed=10 * 2**20, transcendentals=0),
    )(queries, key_rows, value_rows, out_proj, grad_out, band_blocks, column_reach)
    grads = pl.pallas_call(
        result_kernel,
        out_shape=(result,) * 4,
        in_specs=[any_place] * 5,
        out_specs=(any_place,) * 4,
        scratch_shapes=[low(SEQ, 48, 128), low(4, tokens, width), pltpu.SemaphoreType.DMA((11,))],
        compiler_params=pltpu.CompilerParams(vmem_limit_bytes=56 * 2**20),
        cost_estimate=pl.CostEstimate(flops=0, bytes_accessed=8 * 2**20, transcendentals=0),
    )(*parts)
    return (*grads, proj_grad.T)


def solution(mesh):
    tokens = P("seq", "head")
    return jax.shard_map(
        local,
        mesh=mesh,
        in_specs=(tokens, tokens, tokens, P("head", None), tokens, P("seq"), P("seq")),
        out_specs=(tokens, tokens, tokens, tokens, P("head", "seq")),
        check_vma=False,
    )
```

time: 192 us -> 153 us (0.80)
  Pallas kernels: 182 us -> 152 us
  local copies, waits for them, and re-layouts: 8.19 us -> 0.61 us
    pallas_call x1 -> x2, Pallas kernels: 182 us -> 152 us  [the longest x1 148 us: local(): pl.pallas_call(layer_kernel, out_shape=(result, banded, banded, banded, s...]
    unnamed x10 -> x3, local copies, waits for them, and re-layouts: 6.53 us -> 0.61 us
where the time goes in v3:
time: 153 us
  Pallas kernels  152 us (99%)
    pallas_call x1, Pallas kernels, local(): pl.pallas_call(layer_kernel, out_shape=(result, banded, banded, banded, s...  148 us
    pallas_call x1, Pallas kernels, local(): pl.pallas_call(result_kernel, out_shape=(result,) * 4, in_specs=[any_plac...  3.44 us

profile of v3, /device:TPU:16, one launch (start us, length us, event | category | flops | bytes accessed | tf_op | source)
XLA Modules:
  0.0 153.1 jit_solution(1855567912086064734)
XLA Ops:
  0.6 148.4 %shard_map.110 = (bf16[1024,512]{1,0:T(8,128)(2,1)}, bf16[1024,256]{1,0:T(8,128)(2,1)}, bf16[1024,256]{1,0:T(8,128)(2,1)}, bf16[1024,256]{1,0:T(8,128)(2,1)}, bf...) custom-call(bf16[1024,512]{1,0:T(8,128)(2,1)} %q_in.1, bf16[1024,512]{1,0:T(8,128)(2,1)} %k_in.1, bf16[1024,512]{1,0:T(8,128)(2,1)} %v_in.1, ...), custom_call_target="tpu_custom_call" | custom-call | flops 20000000000 | bytes 10485760 | tf_op jit(solution)/shard_map/pallas_call | solution.py:489
  149.0 0.0 copy-start
  149.0 3.4 %shard_map.111 = (bf16[1024,512]{1,0:T(8,128)(2,1)}, bf16[1024,512]{1,0:T(8,128)(2,1)}, bf16[1024,512]{1,0:T(8,128)(2,1)}, bf16[1024,512]{1,0:T(8,128)(2,1)}) custom-call(bf16[1024,512]{1,0:T(8,128)(2,1)} %get-tuple-element.15.out_ref, bf16[1024,256]{1,0:T(8,128)(2,1)} %get-tuple-element.16.dq_ref, bf16[1024,256]{1,0:T(8,128)(2,1)} %get-tuple-element.17.dk_ref, ...), custom_call_target="tpu_custom_call" | custom-call | bytes 8388608 | tf_op jit(solution)/shard_map/pallas_call | solution.py:514
  152.5 0.0 copy-done
  152.5 0.6 copy.13
Async XLA Ops:
  149.0 3.5 %copy-start = (f32[8,512]{1,0:T(8,128)S(1)}, f32[8,512]{1,0:T(8,128)}, u32[]{:S(2)}) copy-start(f32[8,512]{1,0:T(8,128)} %get-tuple-element.24) | copy-start | bytes 49156

commit v4 on v3

--- a/solution.py
+++ b/solution.py
@@ -127,20 +127,25 @@
             device_id=(seq, head if other is None else other), device_id_type=MESH,
         )
 
-    def exchange(start):
-        place = (me // 4) * 2 + core
-
-        def peer(i, side):
-            to = lax.rem(place + i, SEQ // 2)
-            return (to // 2) * 4 + side * 2 + lax.rem(to, 2)
-
-        @pl.loop(1, SEQ // 2)
+    place = (me // 4) * 2 + core
+
+    def peer(i, side):
+        to = lax.rem(place + i, SEQ // 2)
+        return (to // 2) * 4 + side * 2 + lax.rem(to, 2)
+
+    def exchange_near(start):
+        @pl.loop(1, SEQ // 2, unroll=7)
         def _(i):
             start(peer(i, x_hi))
 
-        @pl.loop(0, SEQ // 2)
+    def exchange_far(start):
+        @pl.loop(0, SEQ // 2, unroll=8)
         def _(i):
             start(peer(i, 1 - x_hi))
+
+    def exchange(start):
+        exchange_near(start)
+        exchange_far(start)
 
     def wait_all(src, dst, n):
         everyone = remote(src.at[pl.ds(0, SEQ - 1)], dst.at[pl.ds(0, SEQ - 1)], n, lax.rem(me + 1, SEQ))
@@ -190,12 +195,18 @@
     def _():
         rim[:, :STRIDE, :] = jnp.zeros((2, STRIDE, half), BF16)
 
-    def start(to):
+    reach_core = remote(reach_all.at[me], reach_all.at[me], 3, me + 1 - 2 * core)
+    reach_core.start()
+
+    def send_qkv(to):
         remote(qkv_send.at[to], qkv_recv.at[me], 2, to).start()
-        remote(reach_all.at[me], reach_all.at[me], 3, to).start()
-
-    exchange(start)
+
+    exchange_near(send_qkv)
     qkv_recv[me] = qkv_send[me]
+    reach_core.wait()
+    two = pl.ds(me - core, 2)
+    reach_x = remote(reach_all.at[two], reach_all.at[two], 20, me + 2 - 4 * x_hi)
+    reach_x.start()
 
     mine_c = pl.ds(pl.multiple_of(head * width, 128), width)
     other_c = pl.ds(pl.multiple_of((1 - head) * width, 128), width)
@@ -236,6 +247,13 @@
             att[mine, lanes] = out_t.T.astype(BF16)
             stats[step, 4 * pair : 4 * pair + 4, :] = jnp.concatenate([*rows[0], *rows[1]], axis=0)
 
+    exchange_far(send_qkv)
+    reach_x.wait()
+    four = pl.ds(me - core - 2 * x_hi, 4)
+    for i in range(1, Z):
+        to = seq_at(y, lax.rem(z + i, Z), x_hi, core)
+        remote(reach_all.at[four], reach_all.at[four], 21, to).start()
+
     swap_g.wait()
 
     @pl.loop(0, tokens // TILE)
@@ -249,6 +267,15 @@
         col_d_send[hp * 64 : hp * 64 + 64] = to_messages(d_att[:, lanes])
     exchange(lambda to: remote(col_d_send.at[to], col_d_recv.at[me], 5, to).start())
     col_d_recv[me] = col_d_send[me]
+
+    some = reach_all.at[pl.ds(0, 4 * (Z - 1))]
+    reach_z = remote(some, some, 21, seq_at(y, lax.rem(z + 1, Z), x_hi, core))
+    reach_z.wait_send()
+    reach_z.wait_recv()
+    slab = pl.ds(y * (4 * Z), 4 * Z)
+    for i in range(1, Y):
+        to = seq_at(lax.rem(y + i, Y), z, x_hi, core)
+        remote(reach_all.at[slab], reach_all.at[slab], 22, to).start()
 
     part_w = pl.ds(pl.multiple_of(core * (width // 2), 16), width // 2)
     swap_w = remote(w_ref.at[part_w, other_c], w_other.at[part_w], 1, me, 1 - head)
@@ -310,7 +337,10 @@
 
     band_sum = sum_core(0)
 
-    wait_all(reach_all, reach_all, 3)
+    some = reach_all.at[pl.ds(0, 4 * Z * (Y - 1))]
+    reach_y = remote(some, some, 22, seq_at(lax.rem(y + 1, Y), z, x_hi, core))
+    reach_y.wait_send()
+    reach_y.wait_recv()
     wait_all(qkv_send, qkv_recv, 2)
     for t in range(3):
         wide[t] = qkv_recv[:, 16 * t : 16 * t + 16, :].astype(F32).reshape(16 * SEQ, 128)
@@ -349,8 +379,6 @@
     exchange(lambda to: remote(res_out.at[to], got_out.at[me], 7, to).start())
     got_out[me] = res_out[me]
     band_sum = sum_y(0, band_sum)
-    swap_w.wait()
-    share_w.start()
 
     wait_all(col_d_send, col_d_recv, 5)
     wide[3] = col_d_recv[...].astype(F32).reshape(16 * SEQ, 128)
@@ -366,9 +394,15 @@
 
     for t in range(3):
         res_grad[:, 16 * t : 16 * t + 16, :] = wide[t].reshape(SEQ, 16, 128).astype(BF16)
-    exchange(lambda to: remote(res_grad.at[to], got_grad.at[me], 8, to).start())
+
+    def send_grad(to):
+        remote(res_grad.at[to], got_grad.at[me], 8, to).start()
+
+    exchange(send_grad)
     stores = [store(0, res_grad.at[me], got_grad.at[me])]
     band_sum = sum_x(0, band_sum)
+    swap_w.wait()
+    share_w.start()
 
     wait_all(res_out, got_out, 7)
     for hp in range(2):
@@ -504,7 +538,7 @@
             full(2, Y, Z, XH, CORES, 8, half), full(2, Y, Z, XH, 8, half), full(2, Y, Z, XH, 8, half),
             full(2, Y, Z, XH, 8, half), full(2, Z, XH, 8, half), full(2, Z, 8, half), full(2, Z, 8, half),
             full(2, Z, 8, half),
-            pltpu.SemaphoreType.DMA((20,)), pltpu.SemaphoreType.DMA((20,)), pltpu.SemaphoreType.DMA((10,)),
+            pltpu.SemaphoreType.DMA((23,)), pltpu.SemaphoreType.DMA((23,)), pltpu.SemaphoreType.DMA((10,)),
         ],
         compiler_params=pltpu.CompilerParams(
             collective_id=0, has_side_effects=True, vmem_limit_bytes=56 * 2**20

time: 153 us -> 151 us (0.987)
  Pallas kernels: 152 us -> 148 us
    pallas_call x1, Pallas kernels: 148 us -> 145 us  [local(): pl.pallas_call(layer_kernel, out_shape=(result, banded, banded, banded, s...]
where the time goes in v4:
time: 151 us; the launch traced here: 150 us
  Pallas kernels  148 us (98%)
    pallas_call x1, Pallas kernels, local(): pl.pallas_call(layer_kernel, out_shape=(result, banded, banded, banded, s...  145 us
    pallas_call x1, Pallas kernels, local(): pl.pallas_call(result_kernel, out_shape=(result,) * 4, in_specs=[any_plac...  3.44 us

profile of v4, /device:TPU:16, one launch (start us, length us, event | category | flops | bytes accessed | tf_op | source)
XLA Modules:
  0.0 149.7 jit_solution(2520141871609373616)
XLA Ops:
  0.6 145.0 %shard_map.110 = (bf16[1024,512]{1,0:T(8,128)(2,1)}, bf16[1024,256]{1,0:T(8,128)(2,1)}, bf16[1024,256]{1,0:T(8,128)(2,1)}, bf16[1024,256]{1,0:T(8,128)(2,1)}, bf...) custom-call(bf16[1024,512]{1,0:T(8,128)(2,1)} %q_in.1, bf16[1024,512]{1,0:T(8,128)(2,1)} %k_in.1, bf16[1024,512]{1,0:T(8,128)(2,1)} %v_in.1, ...), custom_call_target="tpu_custom_call" | custom-call | flops 20000000000 | bytes 10485760 | tf_op jit(solution)/shard_map/pallas_call | solution.py:523
  145.7 0.0 copy-start
  145.7 3.4 %shard_map.111 = (bf16[1024,512]{1,0:T(8,128)(2,1)}, bf16[1024,512]{1,0:T(8,128)(2,1)}, bf16[1024,512]{1,0:T(8,128)(2,1)}, bf16[1024,512]{1,0:T(8,128)(2,1)}) custom-call(bf16[1024,512]{1,0:T(8,128)(2,1)} %get-tuple-element.15.out_ref, bf16[1024,256]{1,0:T(8,128)(2,1)} %get-tuple-element.16.dq_ref, bf16[1024,256]{1,0:T(8,128)(2,1)} %get-tuple-element.17.dk_ref, ...), custom_call_target="tpu_custom_call" | custom-call | bytes 8388608 | tf_op jit(solution)/shard_map/pallas_call | solution.py:548
  149.1 0.0 copy-done
  149.1 0.6 copy.13
Async XLA Ops:
  145.7 3.5 %copy-start = (f32[8,512]{1,0:T(8,128)S(1)}, f32[8,512]{1,0:T(8,128)}, u32[]{:S(2)}) copy-start(f32[8,512]{1,0:T(8,128)} %get-tuple-element.24) | copy-start | bytes 49156
